TPU v7x, 256 devices: a whole 4x4x8 slice. The times are simulated.
256 devices in a mesh: rows: 32 (over x_hi, z, core), ch: 8 (over y, x_lo).
Axes of the slice: x: 4 (x_hi: 2, x_lo: 2; x = x_hi * 2 + x_lo), y: 4, z: 8, core: 2. Of those that a mesh axis runs over, the one named last changes fastest.
Arguments:
- fine_in: bfloat16 [48, 6144, 256], P(None, ('rows', 'ch')), may hold values from -6 to 6
- coarse_in: bfloat16 [96, 3072, 128], P('ch', 'rows'), may hold values from -6 to 6
- fine_kernel: bfloat16 [9, 48, 48], replicated, may hold values from -0.3125 to 0.3125
- coarse_kernel: bfloat16 [9, 96, 96], replicated, may hold values from -0.21875 to 0.21875
- up_weight: bfloat16 [48, 96], replicated, may hold values from -0.625 to 0.625
- down_weight: bfloat16 [9, 96, 48], replicated, may hold values from -0.3125 to 0.3125
- fine_cotangent: bfloat16 [48, 6144, 256], P(None, ('rows', 'ch')), may hold values from -6 to 6
- coarse_cotangent: bfloat16 [96, 3072, 128], P(None, ('rows', 'ch')), may hold values from -6 to 6
Outputs:
- joined_fine: bfloat16 [48, 6144, 256], P(None, ('rows', 'ch'))
- joined_coarse: bfloat16 [96, 3072, 128], P(None, ('rows', 'ch'))
- grad_up: float32 [48, 96], replicated
- grad_down: float32 [9, 96, 48], replicated
All inputs are finite; a program needn't handle non-finite values.
Results may differ from a plain program's by a relative error of at most 0.025.
Values may be sent and summed in bfloat16 or wider, within the bound.
A program may use at most 128 MiB of HBM per device.

v0:
```python
import jax
import jax.numpy as jnp
from jax import lax
from jax.sharding import PartitionSpec as P


def with_halo(value, sides, width):
    for axis, dim in sides:
        peers, length = (lax.axis_size(axis), value.shape[dim])
        up = [(i, (i + 1) % peers) for i in range(peers - 1)]
        down = [(j, i) for i, j in up]
        last = lax.slice_in_dim(value, length - width, length, axis=dim)
        first = lax.slice_in_dim(value, 0, width, axis=dim)
        before = lax.ppermute(last, axis, up)
        after = lax.ppermute(first, axis, down)
        value = jnp.concatenate([before, value, after], axis=dim)
    return value


def from_behind(value, axis, steps):
    count = lax.axis_size(axis)
    first, last = (max(0, -steps), min(count, count - steps))
    return lax.ppermute(value, axis, [(source, source + steps) for source in range(first, last)])


def smooth_gate(values):
    return jax.nn.gelu(values, approximate=True)


def conv_rows(weight, padded, row_count):
    col_count = padded.shape[2]
    widened = jnp.pad(padded, ((0, 0), (0, 0), (1, 1)))
    summed = None
    for kernel_tap in range(9):
        row_shift = kernel_tap // 3
        col_shift = kernel_tap % 3
        window = widened[:, row_shift : row_shift + row_count, col_shift : col_shift + col_count]
        partial_value = jnp.einsum(
            "oc,chw->ohw", weight[kernel_tap], window, preferred_element_type=jnp.float32
        )
        summed = partial_value if summed is None else summed + partial_value
    return summed


def shards(
    fine_in,
    coarse_in,
    fine_kernel,
    coarse_kernel,
    up_weight,
    down_weight,
    fine_cotangent,
    coarse_cotangent,
):
    fine_rows = fine_in.shape[1]
    fine_cols = fine_in.shape[2]
    coarse_rows = fine_rows // 2
    coarse_cols = fine_cols // 2
    fine_channels = fine_in.shape[0]
    padded_fine = with_halo(fine_in, ((("rows", "ch"), 1),), 1)
    features_fine = conv_rows(fine_kernel, padded_fine, fine_rows).astype(jnp.bfloat16)
    previous = from_behind(features_fine[:, fine_rows - 1 :, :], ("rows", "ch"), 1)
    local_channels = coarse_in.shape[0]
    strip_rows = coarse_in.shape[1]
    own_kernel = lax.dynamic_slice_in_dim(
        coarse_kernel, lax.axis_index("ch") * local_channels, local_channels, 2
    )
    padded_coarse = with_halo(coarse_in, (("rows", 1),), 1)
    summed_coarse = lax.psum_scatter(
        conv_rows(own_kernel, padded_coarse, strip_rows).astype(jnp.bfloat16),
        "ch",
        scatter_dimension=0,
        tiled=True,
    )
    features_coarse = lax.all_to_all(summed_coarse, "ch", split_axis=1, concat_axis=0, tiled=True)
    lifted = jnp.einsum(
        "oc,chw->ohw", up_weight, features_coarse, preferred_element_type=jnp.float32
    )
    spread = jnp.broadcast_to(
        lifted[:, :, None, :, None], (fine_channels, coarse_rows, 2, coarse_cols, 2)
    )
    pre_fine = features_fine.astype(jnp.float32) + spread.reshape(
        fine_channels, fine_rows, fine_cols
    )
    joined_fine = smooth_gate(pre_fine).astype(jnp.bfloat16)
    stacked = jnp.concatenate([previous, features_fine], axis=1)
    widened = jnp.pad(stacked, ((0, 0), (0, 0), (1, 0)))
    windows = []
    lowered = None
    for kernel_tap in range(9):
        row_shift = kernel_tap // 3
        col_shift = kernel_tap % 3
        window = widened[
            :,
            row_shift : row_shift + 2 * coarse_rows - 1 : 2,
            col_shift : col_shift + 2 * coarse_cols - 1 : 2,
        ]
        windows.append(window)
        partial_value = jnp.einsum(
            "oc,chw->ohw", down_weight[kernel_tap], window, preferred_element_type=jnp.float32
        )
        lowered = partial_value if lowered is None else lowered + partial_value
    pre_coarse = features_coarse.astype(jnp.float32) + lowered
    joined_coarse = smooth_gate(pre_coarse).astype(jnp.bfloat16)
    pullback_fine = jax.vjp(smooth_gate, pre_fine)[1]
    slope_fine = pullback_fine(fine_cotangent.astype(jnp.float32))[0].astype(jnp.bfloat16)
    pullback_coarse = jax.vjp(smooth_gate, pre_coarse)[1]
    slope_coarse = pullback_coarse(coarse_cotangent.astype(jnp.float32))[0].astype(jnp.bfloat16)
    pooled = (
        slope_fine.astype(jnp.float32)
        .reshape(fine_channels, coarse_rows, 2, coarse_cols, 2)
        .sum(axis=(2, 4))
        .astype(jnp.bfloat16)
    )
    up_terms = jnp.einsum(
        "ohw,chw->oc", pooled, features_coarse, preferred_element_type=jnp.float32
    )
    down_terms = jnp.stack(
        [
            jnp.einsum("ohw,chw->oc", slope_coarse, window, preferred_element_type=jnp.float32)
            for window in windows
        ]
    )
    grad_up, grad_down = lax.psum((up_terms, down_terms), ("rows", "ch"))
    return (joined_fine, joined_coarse, grad_up, grad_down)


def solution(mesh):
    return jax.shard_map(
        shards,
        mesh=mesh,
        in_specs=(
            P(None, ("rows", "ch"), None),
            P("ch", "rows", None),
            P(),
            P(),
            P(),
            P(),
            P(None, ("rows", "ch"), None),
            P(None, ("rows", "ch"), None),
        ),
        out_specs=(P(None, ("rows", "ch"), None), P(None, ("rows", "ch"), None), P(), P()),
        check_vma=False,
    )
```

profile of v0, /device:TPU:1, one launch (start us, length us, event | category | flops | bytes accessed | tf_op | source)
XLA Modules:
  0.0 475.6 jit_solution(5300716745001875934)
XLA Ops:
  8.4 4.9 %collective-permute-start.2 = (bf16[12,1,128]{2,0,1:T(8,128)(2,1)S(1)}, bf16[12,1,128]{2,0,1:T(8,128)(2,1)S(1)}, u32[]{:S(2)}, u32[]{:S(2)}) collective-permute-start(bf16[12,1,128]{2,0,1:T(8,128)(2,1)S(1)} %get-tuple-element.30), channel_id=1, source_target_pairs={{0,8},{8,16},{16,24},{24,32},{32,40},{40,48},{48,56},{56,64},{64,7... | collective-permute-start | bytes 9224 | tf_op jit(solution)/shard_map/ppermute | solution.py:14
  15.3 3.9 fusion.80
  38.5 12.5 %add_convert_fusion = bf16[96,96,128]{2,0,1:T(8,128)(2,1)} fusion(f32[96,96,128]{2,0,1:T(8,128)} %fusion.66, f32[96,96,128]{2,0,1:T(8,128)} %fusion.68, f32[96,96,128]{2,0,1:T(8,128)} %fusion.70, f32[96,96,128]{2,0,1:T(8,128)S(1)} %bitcast.238, f32[96,96,128]{2,0,1:T(8,128)} %fusion.72, f32[96,96,128]{2,0,1:T(8,128)} %fusion.74, ...), kind=kOutput, calls=%fused_computation | convolution fusion | flops 38928384 | bytes 40525832 | tf_op jit(solution)/shard_map/oc,chw->ohw/dot_general | solution.py:38
  51.0 4.0 copy.102
  56.2 3.1 collective-permute-start
  59.3 4.5 collective-permute-start.1
  70.1 48.5 %reduce-scatter.2.cloned.1.call-done = bf16[12,96,128]{2,1,0:T(8,128)(2,1)} async-done(((bf16[96,96,128]{2,1,0:T(8,128)(2,1)}), bf16[12,96,128]{2,1,0:T(8,128)(2,1)}) %reduce-scatter.2.cloned.1.call-update) | async-done | bytes 294928 | tf_op jit(solution)/shard_map/reduce_scatter | solution.py:69
  120.5 3.5 all-to-all-start
  127.0 4.8 %all-to-all-done = bf16[12,96,128]{2,0,1:T(8,128)(2,1)S(1)} async-done(((bf16[12,96,128]{2,0,1:T(8,128)(2,1)}), bf16[12,96,128]{2,0,1:T(8,128)(2,1)S(1)}, u32[]{:S(2)}, u32[]{:S(2)}) %all-to-all-start) | async-done | bytes 294944 | tf_op jit(solution)/shard_map/all_to_all | solution.py:75
  133.2 4.1 broadcast_in_dim.2
  137.4 3.1 copy.107
  140.5 5.6 %fusion.15 = (bf16[48,24,256]{2,0,1:T(8,128)(2,1)}, bf16[48,24,256]{2,0,1:T(8,128)(2,1)}, bf16[48,24,256]{2,0,1:T(8,128)(2,1)S(1)}) fusion(f32[48,24,256]{2,0,1:T(8,128)} %copy.107, bf16[48,24,256]{2,1,0:T(8,128)(2,1)} %param.14, f32[48,24,256]{2,0,1:T(8,128)} %convolution_bitcast_fusion, f32[48,24,256]{2,0,1:T(8,128)} %convolution_bitcast_fusion.1, ...), kind=kOutput, calls=%fused_computation.40 | convolution fusion | flops 37748736 | bytes 11218944 | tf_op jit(solution)/shard_map/oc,chw->ohw/dot_general | solution.py:38
  151.2 3.8 reduce
  155.4 5.9 %slice.224 = bf16[48,12,128]{2,0,1:T(8,128)(2,1)S(1)} slice(bf16[48,25,257]{2,0,1:T(8,128)(2,1)S(1)} %fusion.40), slice={[0:48:1], [0:23:2], [1:256:2]} | slice | bytes 294912 | tf_op jit(solution)/shard_map/slice | solution.py:93
  161.4 5.9 %slice.222 = bf16[48,12,128]{2,0,1:T(8,128)(2,1)S(1)} slice(bf16[48,25,257]{2,0,1:T(8,128)(2,1)S(1)} %fusion.40), slice={[0:48:1], [0:23:2], [0:255:2]} | slice | bytes 294912 | tf_op jit(solution)/shard_map/slice | solution.py:93
  167.3 6.0 %slice.226 = bf16[48,12,128]{2,0,1:T(8,128)(2,1)S(1)} slice(bf16[48,25,257]{2,0,1:T(8,128)(2,1)S(1)} %fusion.40), slice={[0:48:1], [0:23:2], [2:257:2]} | slice | bytes 294912 | tf_op jit(solution)/shard_map/slice | solution.py:93
  173.3 5.9 %slice.228 = bf16[48,12,128]{2,0,1:T(8,128)(2,1)S(1)} slice(bf16[48,25,257]{2,0,1:T(8,128)(2,1)S(1)} %fusion.40), slice={[0:48:1], [1:24:2], [0:255:2]} | slice | bytes 294912 | tf_op jit(solution)/shard_map/slice | solution.py:93
  179.3 5.9 %slice.230 = bf16[48,12,128]{2,0,1:T(8,128)(2,1)S(1)} slice(bf16[48,25,257]{2,0,1:T(8,128)(2,1)S(1)} %fusion.40), slice={[0:48:1], [1:24:2], [1:256:2]} | slice | bytes 294912 | tf_op jit(solution)/shard_map/slice | solution.py:93
  185.2 6.0 %slice.232 = bf16[48,12,128]{2,0,1:T(8,128)(2,1)S(1)} slice(bf16[48,25,257]{2,0,1:T(8,128)(2,1)S(1)} %fusion.40), slice={[0:48:1], [1:24:2], [2:257:2]} | slice | bytes 294912 | tf_op jit(solution)/shard_map/slice | solution.py:93
  191.2 6.2 %slice.234 = bf16[48,12,128]{2,0,1:T(8,128)(2,1)S(1)} slice(bf16[48,25,257]{2,0,1:T(8,128)(2,1)S(1)} %fusion.40), slice={[0:48:1], [2:25:2], [0:255:2]} | slice | bytes 294912 | tf_op jit(solution)/shard_map/slice | solution.py:93
  197.4 6.2 %slice.236 = bf16[48,12,128]{2,0,1:T(8,128)(2,1)S(1)} slice(bf16[48,25,257]{2,0,1:T(8,128)(2,1)S(1)} %fusion.40), slice={[0:48:1], [2:25:2], [1:256:2]} | slice | bytes 294912 | tf_op jit(solution)/shard_map/slice | solution.py:93
  203.6 6.4 %slice.238 = bf16[48,12,128]{2,0,1:T(8,128)(2,1)S(1)} slice(bf16[48,25,257]{2,0,1:T(8,128)(2,1)S(1)} %fusion.40), slice={[0:48:1], [2:25:2], [2:257:2]} | slice | bytes 294912 | tf_op jit(solution)/shard_map/slice | solution.py:93
  217.1 81.5 %psum.14 = f32[48,96]{1,0:T(8,128)} all-reduce(f32[48,96]{1,0:T(8,128)S(1)} %convolution_bitcast_fusion.5), channel_id=1, replica_groups=mesh['rows'=32,'ch'=8] {'rows','ch'}, use_global_device_ids=true, to_apply=%region_2.3 | all-reduce | flops 4608 | bytes 36864 | tf_op jit(solution)/shard_map/psum | solution.py:124
  298.7 168.5 %all-reduce.5.cloned.1.call-done = f32[9,96,48]{1,2,0:T(8,128)} async-done(((f32[9,96,48]{1,2,0:T(8,128)}), f32[9,96,48]{1,2,0:T(8,128)}) %all-reduce.5.cloned.1.call-update) | async-done | bytes 165904 | tf_op jit(solution)/shard_map/psum | solution.py:124
  (94 shorter events, 50.0 us)
Async XLA Ops:
  7.2 8.1 %copy-start = (bf16[9,96,96]{2,1,0:T(8,128)(2,1)S(1)}, bf16[9,96,96]{2,1,0:T(8,128)(2,1)}, u32[]{:S(2)}) copy-start(bf16[9,96,96]{2,1,0:T(8,128)(2,1)} %param.11) | copy-start | bytes 497668
  7.2 111.4 %reduce-scatter.2.cloned.1.call-start = ((), (), s32[]{:S(2)}) async-start(), calls=%async_computation.2 | async-start | bytes 2654208 | tf_op jit(solution)/shard_map/reduce_scatter | solution.py:69
  8.4 10.8 %copy-start.3 = (bf16[12,96,128]{2,0,1:T(8,128)(2,1)}, bf16[12,96,128]{2,0,1:T(8,128)(2,1)S(1)}, u32[]{:S(2)}) copy-start(bf16[12,96,128]{2,0,1:T(8,128)(2,1)S(1)} %copy.96) | copy-start | bytes 884740
  8.4 10.8 %collective-permute-start.2 = (bf16[12,1,128]{2,0,1:T(8,128)(2,1)S(1)}, bf16[12,1,128]{2,0,1:T(8,128)(2,1)S(1)}, u32[]{:S(2)}, u32[]{:S(2)}) collective-permute-start(bf16[12,1,128]{2,0,1:T(8,128)(2,1)S(1)} %get-tuple-element.30), channel_id=1, source_target_pairs={{0,8},{8,16},{16,24},{24,32},{32,40},{40,48},{48,56},{56,64},{64,7... | collective-permute-start | bytes 9224 | tf_op jit(solution)/shard_map/ppermute | solution.py:14
  13.3 5.8 %collective-permute-start.3 = (bf16[12,1,128]{2,0,1:T(8,128)(2,1)S(1)}, bf16[12,1,128]{2,0,1:T(8,128)(2,1)S(1)}, u32[]{:S(2)}, u32[]{:S(2)}) collective-permute-start(bf16[12,1,128]{2,0,1:T(8,128)(2,1)S(1)} %get-tuple-element.31), channel_id=1, source_target_pairs={{8,0},{16,8},{24,16},{32,24},{40,32},{48,40},{56,48},{64,56},{72,6... | collective-permute-start | bytes 9224 | tf_op jit(solution)/shard_map/ppermute | solution.py:15
  19.6 9.8 %copy-start.2 = (bf16[12,98,130]{2,0,1:T(8,128)(2,1)}, bf16[12,98,130]{2,0,1:T(8,128)(2,1)S(1)}, u32[]{:S(2)}) copy-start(bf16[12,98,130]{2,0,1:T(8,128)(2,1)S(1)} %fusion.42) | copy-start | bytes 917284
  29.4 3.1 copy-start.4
  29.4 9.0 %slice-start = ((s8[4718592]{0:T(1024)(128)(4,1)}), s8[4194304]{0:T(1024)(128)(4,1)S(1)}, s32[]{:S(2)}) async-start(s8[4718592]{0:T(1024)(128)(4,1)} %bitcast.237), calls=%async_computation.4 | async-start | bytes 8388608
  32.5 6.0 %slice-start.1 = ((s8[4718592]{0:T(1024)(128)(4,1)}), s8[524288]{0:T(1024)(128)(4,1)S(1)}, s32[]{:S(2)}) async-start(s8[4718592]{0:T(1024)(128)(4,1)} %bitcast.237), calls=%async_computation.5 | async-start | bytes 1048576
  55.0 1.1 copy-start.8
  56.1 7.8 %copy-start.10 = (bf16[9,48,48]{2,1,0:T(8,128)(2,1)S(1)}, bf16[9,48,48]{2,1,0:T(8,128)(2,1)}, u32[]{:S(2)}) copy-start(bf16[9,48,48]{2,1,0:T(8,128)(2,1)} %param.10) | copy-start | bytes 124420
  56.2 8.0 %collective-permute-start = (bf16[48,1,256]{2,0,1:T(8,128)(2,1)S(1)}, bf16[48,1,256]{2,0,1:T(8,128)(2,1)S(1)}, u32[]{:S(2)}, u32[]{:S(2)}) collective-permute-start(bf16[48,1,256]{2,0,1:T(8,128)(2,1)S(1)} %get-tuple-element.28), channel_id=1, source_target_pairs={{0,1},{1,2},{2,3},{3,4},{4,5},{5,6},{6,7},{7,8},{8,9},{9,10},{10,1... | collective-permute-start | bytes 73736 | tf_op jit(solution)/shard_map/ppermute | solution.py:14
  59.3 5.5 %collective-permute-start.1 = (bf16[48,1,256]{2,0,1:T(8,128)(2,1)S(1)}, bf16[48,1,256]{2,0,1:T(8,128)(2,1)S(1)}, u32[]{:S(2)}, u32[]{:S(2)}) collective-permute-start(bf16[48,1,256]{2,0,1:T(8,128)(2,1)S(1)} %get-tuple-element.29), channel_id=1, source_target_pairs={{1,0},{2,1},{3,2},{4,3},{5,4},{6,5},{7,6},{8,7},{9,8},{10,9},{11,1... | collective-permute-start | bytes 73736 | tf_op jit(solution)/shard_map/ppermute | solution.py:15
  120.5 11.3 %all-to-all-start = ((bf16[12,96,128]{2,0,1:T(8,128)(2,1)}), bf16[12,96,128]{2,0,1:T(8,128)(2,1)S(1)}, u32[]{:S(2)}, u32[]{:S(2)}) async-start(bf16[12,96,128]{2,0,1:T(8,128)(2,1)} %copy.103), calls=%async_computation.1 | async-start | bytes 786432 | tf_op jit(solution)/shard_map/all_to_all | solution.py:75
  123.9 343.2 %all-reduce.5.cloned.1.call-start = ((), (), s32[]{:S(2)}) async-start(), calls=%async_computation.3 | async-start | bytes 442368 | tf_op jit(solution)/shard_map/psum | solution.py:124
  127.0 4.9 %copy-start.12 = (bf16[48,96]{1,0:T(8,128)(2,1)S(1)}, bf16[48,96]{1,0:T(8,128)(2,1)}, u32[]{:S(2)}) copy-start(bf16[48,96]{1,0:T(8,128)(2,1)} %param.12) | copy-start | bytes 27652
  146.1 2.4 copy-start.5
  146.1 4.1 copy-start.7
  146.1 8.9 %collective-permute-start.4 = (bf16[48,1,256]{2,0,1:T(8,128)(2,1)S(1)}, bf16[48,1,256]{2,0,1:T(8,128)(2,1)S(1)}, u32[]{:S(2)}, u32[]{:S(2)}) collective-permute-start(bf16[48,1,256]{2,0,1:T(8,128)(2,1)S(1)} %slice.256), channel_id=1, source_target_pairs={{0,1},{1,2},{2,3},{3,4},{4,5},{5,6},{6,7},{7,8},{8,9},{9,10},{10,1... | collective-permute-start | bytes 73736 | tf_op jit(solution)/shard_map/ppermute | solution.py:23
  151.2 3.8 copy-start.6
  161.4 48.7 %copy-start.11 = (bf16[9,96,48]{1,2,0:T(8,128)(2,1)S(1)}, bf16[9,96,48]{1,2,0:T(8,128)(2,1)}, u32[]{:S(2)}) copy-start(bf16[9,96,48]{1,2,0:T(8,128)(2,1)} %param.13) | copy-start | bytes 248836
  211.8 1.0 copy-start.13
  215.5 253.3 %copy-start.1 = (bf16[9,96,96]{2,1,0:T(8,128)(2,1)S(1)}, bf16[9,96,96]{2,1,0:T(8,128)(2,1)}, u32[]{:S(2)}) copy-start(bf16[9,96,96]{2,1,0:T(8,128)(2,1)} %param.11) | copy-start | bytes 497668
  216.1 0.7 copy-start.9
Sparse Core Ops, SparseCore 0:
  55.2 63.4 reduce-scatter.1
  217.0 250.1 all-reduce.4
where the time goes:
time: 476 us
  waiting for transfers between devices  222 us (47%)
  blocking collectives  81.5 us (17%)
  local copies, waits for them, and re-layouts  76.7 us (16%)
  matrix products  54.6 us (11%)
  starting transfers between devices  20.6 us (4%)
  between operations  14.6 us (3%)
  other arithmetic  5.09 us (1%)
    psum x1, waiting for transfers between devices, shards(): grad_up, grad_down = lax.psum((up_terms, down_terms), ('rows', 'ch'))  168 us
    psum x1, blocking collectives, shards(): grad_up, grad_down = lax.psum((up_terms, down_terms), ('rows', 'ch'))  81.5 us
    slice x9, local copies, waits for them, and re-layouts, shards(): widened[:, row_shift:row_shift + 2 * coarse_rows - 1:2, col_shift:col_shi...  54.5 us
    dot_general x18, matrix products, conv_rows(): jnp.einsum('oc,chw->ohw', weight[kernel_tap], window, preferred_element_t...  48.7 us
    reduce_scatter x1, waiting for transfers between devices, shards(): lax.psum_scatter(conv_rows(own_kernel, padded_coarse, strip_rows).astype(...  48.5 us
  transfers between devices with their start and end apart: 8, of which 4 were waited for; matrix products, arithmetic and copies ran while one was open for 4% of the time, Pallas kernels for 0%

commit v1 on v0

v1 whole, which is shorter than its diff:
```python
import functools

import jax
import jax.numpy as jnp
from jax import lax
from jax.experimental import pallas as pl
from jax.experimental.pallas import tpu as pltpu
from jax.sharding import PartitionSpec as P

BF = jnp.bfloat16
F32 = jnp.float32
MESH = pl.DeviceIdType.MESH


def dot(a, b):
    return lax.dot_general(a, b, (((1,), (0,)), ((), ())), preferred_element_type=F32)


def dot_nt(a, b):
    return lax.dot_general(a, b, (((1,), (1,)), ((), ())), preferred_element_type=F32)


def one_hot(rows, cols, match):
    r = lax.broadcasted_iota(jnp.int32, (rows, cols), 0)
    c = lax.broadcasted_iota(jnp.int32, (rows, cols), 1)
    return jnp.where(match(r, c), 1.0, 0.0).astype(BF)


def split_columns():
    return one_hot(256, 512, lambda r, c: r == 2 * (c % 128) + c // 128 - 1)


def join_columns():
    return one_hot(256, 256, lambda r, c: c == 2 * (r % 128) + r // 128)


def gate(v):
    k, m = 0.7978845608028654, 0.044715
    q = v * v
    t = jnp.tanh(v * (k + (k * m) * q))
    half = 0.5 + 0.5 * t
    joined = v * half
    slope = half + (0.5 * v) * (1.0 - t * t) * (k + (3 * k * m) * q)
    return joined, slope


def prep_weights(fk, ck, dw, tb, wc, dm):
    fka = [fk[3 * a : 3 * a + 3].reshape(144, 48) for a in range(3)]
    for r in range(3):
        acc = None
        for a in range(3):
            d = dot(fka[a], one_hot(48, 240, lambda i, j: j == (r + a) * 48 + i))
            acc = d if acc is None else acc + d
        acc = acc.astype(BF)
        for b in range(3):
            tb[b, 48 * r : 48 * r + 48, :] = acc[48 * b : 48 * b + 48]
    place = one_hot(96, 128, lambda i, j: j == (i // 12) * 16 + i % 12)
    wide = dot(ck[...].reshape(864, 96), place).astype(BF)
    for t in range(9):
        a, b = t // 3, t % 3
        wc[96 * b : 96 * b + 96, 128 * a : 128 * a + 128] = wide[96 * t : 96 * t + 96]
    stacked = jnp.concatenate([dw[3 * a + b] for b in range(3) for a in range(3)], axis=0)
    dm[...] = stacked.T


def prep_coarse(ci, z):
    v = jnp.concatenate([ci[...], jnp.zeros((4, 96, 128), BF)], axis=0)
    z[1:97] = jnp.swapaxes(v, 0, 1)
    z[0] = jnp.zeros((16, 128), BF)
    z[97] = jnp.zeros((16, 128), BF)


def spread_fine(rows, u, at):
    n = rows.shape[0]
    u[at * 48 : (at + n) * 48, :] = dot(rows.reshape(n * 48, 256), split_columns()).astype(BF)


def store_features(g, at, out):
    lane = lax.broadcasted_iota(jnp.int32, (48, 128), 1)
    shifted = jnp.where(lane == 0, 0.0, pltpu.roll(out[:, 128:], 1, 1))
    g[at * 48 : at * 48 + 48, :] = jnp.concatenate([shifted, out], axis=1).astype(BF)


def fine_group(tb, u, g, group):
    acc = None
    base = (3 * group + 1) * 48
    for b in range(3):
        d = dot(tb[b], u[base : base + 240, 128 * b : 128 * b + 256])
        acc = d if acc is None else acc + d
    for r in range(3):
        store_features(g, 3 * group + r + 1, acc[48 * r : 48 * r + 48])


def fine_before(tb, u, g, keep):
    acc = None
    for b in range(3):
        d = dot(tb[b, 0:48, 0:144], u[0:144, 128 * b : 128 * b + 256])
        acc = d if acc is None else acc + d
    store_features(g, 0, jnp.where(keep, acc, 0.0))


def coarse_pair(wc, r, fc, p):
    i = 2 * p
    rows = jnp.concatenate(
        [r[i : i + 3].reshape(384, 128), r[i + 1 : i + 4].reshape(384, 128)], axis=1
    )
    y = dot(wc[...], rows)
    lane = lax.broadcasted_iota(jnp.int32, (96, 128), 1)
    for s in range(2):
        left = y[0:96, 128 * s : 128 * s + 128]
        mid = y[96:192, 128 * s : 128 * s + 128]
        right = y[192:288, 128 * s : 128 * s + 128]
        left = jnp.where(lane == 0, 0.0, pltpu.roll(left, 1, 1))
        right = jnp.where(lane == 127, 0.0, pltpu.roll(right, 127, 1))
        fc[p, :, 128 * s : 128 * s + 128] = (left + mid + right).astype(BF)


def windows(g, p):
    cols = []
    for i in (2 * p, 2 * p + 1):
        taps = [g[2 * i * 48 : (2 * i + 3) * 48, 128 * b : 128 * b + 128] for b in range(3)]
        cols.append(jnp.concatenate(taps, axis=0))
    return jnp.concatenate(cols, axis=1)


def join_pair(up, dm, g, fc, fcot, ccot, jf, jc, p):
    f = fc[p]
    lifted = dot(up[...], f)
    pooled = []
    for s in range(2):
        one = lifted[:, 128 * s : 128 * s + 128]
        both = jnp.concatenate([one, one], axis=1)
        total = None
        for a in range(2):
            h = 2 * (2 * p + s) + a
            pre = g[(h + 1) * 48 : (h + 2) * 48, 128:384].astype(F32) + both
            joined, slope = gate(pre)
            jf[h * 48 : (h + 1) * 48, :] = joined.astype(BF)
            term = (fcot[h * 48 : (h + 1) * 48, :].astype(F32) * slope).astype(BF).astype(F32)
            total = term if total is None else total + term
        pooled.append(total[:, :128] + total[:, 128:])
    pooled = jnp.concatenate(pooled, axis=1).astype(BF)
    gu = dot_nt(pooled, f)
    w = windows(g, p)
    pre = f.astype(F32) + dot(dm[...], w)
    joined, slope = gate(pre)
    for s in range(2):
        jc[2 * p + s] = joined[:, 128 * s : 128 * s + 128].astype(BF)
    cc = jnp.concatenate([ccot[2 * p], ccot[2 * p + 1]], axis=1).astype(F32)
    gd = dot_nt(w, (cc * slope).astype(BF))
    return gu, gd


def pack(gu, gd):
    rows = jnp.concatenate([gd, gu], axis=0)
    wide = jnp.concatenate([rows, jnp.zeros((480, 32), F32)], axis=1)
    tail = wide[384:480]
    lane = lax.broadcasted_iota(jnp.int32, (96, 128), 1)
    parts = []
    for k in range(4):
        head = wide[96 * k : 96 * k + 96]
        if k < 3:
            head = jnp.where(lane < 96, head, pltpu.roll(tail, 96 - 32 * k, 1))
        parts.append(head)
    return jnp.concatenate(parts, axis=0).reshape(16, 24, 128)


def unpack(total, grad_up, grad_down):
    flat = total.reshape(384, 128)
    lane = lax.broadcasted_iota(jnp.int32, (96, 128), 1)
    tail = None
    for k in range(3):
        moved = pltpu.roll(flat[96 * k : 96 * k + 96], (32 + 32 * k) % 128, 1)
        tail = moved if tail is None else jnp.where(lane < 32 * k, tail, moved)
    rows = jnp.concatenate([flat, tail], axis=0)[:, :96]
    for b in range(3):
        for a in range(3):
            k = 3 * b + a
            grad_down[3 * a + b] = rows[48 * k : 48 * k + 48]
    grad_up[...] = rows[432:480]


def kernel(
    nr, nc, x_h, ci_h, fk_h, ck_h, up_h, dw_h, fcot_h, ccot_h,
    jf_o, jc_o, gu_o, gd_o,
    x, ci, fk, ck, up, dw, fcot, ccot, in_sem, out_sem,
    tb, wc, dm, z, t, u, g, rr, fc, fct, jf, jft, jc, gu_v, gd_v,
    top, bot, hf, acc, s1, s2, s3,
    a2a_s, a2a_r, edge_s, edge_r, fine_s, fine_r, ar_s, ar_r,
):
    r = lax.axis_index("rows")
    c = lax.axis_index("ch")
    na = nr // 2
    nb = 2 * nc
    alpha = lax.rem(r, na)
    x_hi = r // na
    beta = x_hi * nc + c

    def in_a(d):
        k = lax.rem(alpha + d, na)
        return k, (x_hi * na + k, c)

    def in_b(d):
        k = lax.rem(beta + d, nb)
        return k, ((k // nc) * na + alpha, lax.rem(k, nc))

    loads = [
        pltpu.make_async_copy(src, dst, in_sem.at[k])
        for k, (src, dst) in enumerate(
            [(ci_h, ci), (x_h, x), (fk_h, fk), (ck_h, ck), (dw_h, dw), (up_h, up), (fcot_h, fcot), (ccot_h, ccot)]
        )
    ]
    for load in loads:
        load.start()

    barrier = pltpu.get_barrier_semaphore()

    def greet(device):
        pl.semaphore_signal(barrier, inc=1, device_id=device, device_id_type=MESH)

    @pl.loop(1, na)
    def _(d):
        greet(in_a(d)[1])

    @pl.loop(1, nb)
    def _(d):
        greet(in_b(d)[1])

    first_row, last_row = r == 0, r == nr - 1
    has_above, has_below = jnp.logical_not(first_row), jnp.logical_not(last_row)
    is_first = jnp.logical_and(c == 0, has_above)
    is_last = jnp.logical_and(c == nc - 1, has_below)

    @pl.when(has_below)
    def _():
        greet((r + 1, 0))

    @pl.when(has_above)
    def _():
        greet((r - 1, nc - 1))

    @pl.when(is_first)
    def _():
        @pl.loop(0, nc)
        def _(k):
            greet((r - 1, k))

    @pl.when(is_last)
    def _():
        @pl.loop(0, nc)
        def _(k):
            greet((r + 1, k))

    loads[0].wait()
    prep_coarse(ci, z)
    rr[:, pl.ds(c, 1)] = z[pl.ds(12 * c, 14)].reshape(14, 1, 16, 128)
    loads[1].wait()
    t[...] = jnp.swapaxes(x[...], 0, 1)

    one = jnp.int32(1)
    zero = jnp.int32(0)
    peers = na + nb - 2
    peers = peers + jnp.where(has_below, one, zero) + jnp.where(has_above, one, zero)
    peers = peers + jnp.where(is_first, nc * one, zero) + jnp.where(is_last, nc * one, zero)
    pl.semaphore_wait(barrier, peers)

    def a2a(d):
        peer = lax.rem(c + d, nc)
        return pltpu.make_async_remote_copy(
            src_ref=z.at[pl.ds(12 * peer, 14)],
            dst_ref=rr.at[:, c],
            send_sem=a2a_s.at[d],
            recv_sem=a2a_r.at[d],
            device_id=(r, peer),
            device_id_type=MESH,
        )

    @pl.loop(1, nc)
    def _(d):
        a2a(d).start()

    def edge(k, src, dst, device):
        return pltpu.make_async_remote_copy(
            src_ref=src, dst_ref=dst, send_sem=edge_s.at[k], recv_sem=edge_r.at[k, c],
            device_id=device, device_id_type=MESH,
        )

    edge_down = edge(0, z.at[96], top.at[c], (r + 1, 0))
    edge_up = edge(1, z.at[1], bot.at[c], (r - 1, nc - 1))

    @pl.when(has_below)
    def _():
        edge_down.start()

    @pl.when(has_above)
    def _():
        edge_up.start()

    wraps_down = c == nc - 1
    wraps_up = c == 0
    has_next = jnp.logical_not(jnp.logical_and(wraps_down, last_row))
    has_prev = jnp.logical_not(jnp.logical_and(wraps_up, first_row))
    next_dev = (r + jnp.where(wraps_down, one, zero), lax.rem(c + 1, nc))
    prev_dev = (r - jnp.where(wraps_up, one, zero), lax.rem(c + nc - 1, nc))

    def halo(k, src, dst, device):
        return pltpu.make_async_remote_copy(
            src_ref=src, dst_ref=dst, send_sem=fine_s.at[k], recv_sem=fine_r.at[k],
            device_id=device, device_id_type=MESH,
        )

    fine_down = halo(0, t.at[pl.ds(22, 2)], hf.at[pl.ds(0, 2)], next_dev)
    fine_up = halo(1, t.at[pl.ds(0, 1)], hf.at[pl.ds(2, 1)], prev_dev)

    @pl.when(has_next)
    def _():
        fine_down.start()

    @pl.when(has_prev)
    def _():
        fine_up.start()

    for load in loads[2:5]:
        load.wait()
    prep_weights(fk, ck, dw, tb, wc, dm)
    spread_fine(t[...], u, 2)
    for k in range(1, 7):
        fine_group(tb, u, g, k)
    for load in loads[5:]:
        load.wait()
    fct[...] = dot(
        jnp.swapaxes(fcot[...], 0, 1).reshape(1152, 256), split_columns()[:, 128:384]
    ).astype(BF)

    @pl.when(has_prev)
    def _():
        fine_down.wait_recv()
        spread_fine(hf[0:2], u, 0)

    @pl.when(jnp.logical_not(has_prev))
    def _():
        u[0:96, :] = jnp.zeros((96, 512), BF)

    @pl.when(has_next)
    def _():
        fine_up.wait_recv()
        spread_fine(hf[2:3], u, 26)

    @pl.when(jnp.logical_not(has_next))
    def _():
        u[26 * 48 : 27 * 48, :] = jnp.zeros((48, 512), BF)

    fine_before(tb, u, g, has_prev)
    fine_group(tb, u, g, 0)
    fine_group(tb, u, g, 7)

    @pl.loop(1, nc)
    def _(d):
        source = lax.rem(c - d + nc, nc)
        pltpu.make_async_remote_copy(
            src_ref=z.at[pl.ds(0, 14)],
            dst_ref=rr.at[:, source],
            send_sem=a2a_s.at[d],
            recv_sem=a2a_r.at[d],
            device_id=(r, source),
            device_id_type=MESH,
        ).wait_recv()

    def edge_wait(k, buf, row):
        @pl.loop(0, nc)
        def _(j):
            pltpu.make_async_remote_copy(
                src_ref=z.at[0], dst_ref=buf.at[j], send_sem=edge_s.at[k], recv_sem=edge_r.at[k, j],
                device_id=(r, c), device_id_type=MESH,
            ).wait_recv()

        rr[row] = buf[...]

    @pl.when(is_first)
    def _():
        edge_wait(0, top, 0)

    @pl.when(is_last)
    def _():
        edge_wait(1, bot, 13)

    for p in range(6):
        coarse_pair(wc, rr, fc, p)
    gu = gd = None
    for p in range(6):
        a, b = join_pair(up, dm, g, fc, fct, ccot, jf, jc, p)
        gu = a if gu is None else gu + a
        gd = b if gd is None else gd + b

    acc[...] = pack(gu, gd).astype(acc.dtype)

    def swap(stage, d, src, dst, device):
        return pltpu.make_async_remote_copy(
            src_ref=src, dst_ref=dst, send_sem=ar_s.at[stage, d], recv_sem=ar_r.at[stage, d],
            device_id=device, device_id_type=MESH,
        )

    @pl.loop(1, nb)
    def _(d):
        k, device = in_b(d)
        swap(0, d, acc.at[k], s1.at[d], device).start()

    stores = [pltpu.make_async_copy(jft, jf_o, out_sem.at[0]), pltpu.make_async_copy(jc, jc_o, out_sem.at[1])]
    stores[1].start()
    jft[...] = jnp.swapaxes(dot(jf[...], join_columns()).astype(BF).reshape(24, 48, 256), 0, 1)
    stores[0].start()

    @pl.loop(1, nb)
    def _(d):
        swap(0, d, acc.at[0], s1.at[d], (r, c)).wait_recv()

    part = acc[beta].astype(F32)
    for d in range(1, nb):
        part = part + s1[d].astype(F32)
    s2[alpha] = part.astype(s2.dtype)

    @pl.loop(1, na)
    def _(d):
        swap(1, d, s2.at[alpha], s2.at[alpha], in_a(d)[1]).start()

    @pl.loop(1, na)
    def _(d):
        k = lax.rem(alpha - d + na, na)
        swap(1, d, s2.at[alpha], s2.at[k], (r, c)).wait_recv()

    part = s2[0].astype(F32)
    for k in range(1, na):
        part = part + s2[k].astype(F32)
    s3[beta] = part.astype(s3.dtype)

    @pl.loop(1, nb)
    def _(d):
        swap(2, d, s3.at[beta], s3.at[beta], in_b(d)[1]).start()

    @pl.loop(1, nb)
    def _(d):
        k = lax.rem(beta - d + nb, nb)
        swap(2, d, s3.at[beta], s3.at[k], (r, c)).wait_recv()

    unpack(s3[...].astype(F32), gu_v, gd_v)
    grads = [pltpu.make_async_copy(gu_v, gu_o, out_sem.at[2]), pltpu.make_async_copy(gd_v, gd_o, out_sem.at[3])]
    for store in grads:
        store.start()

    @pl.loop(1, nc)
    def _(d):
        a2a(d).wait_send()

    @pl.when(has_below)
    def _():
        edge_down.wait_send()

    @pl.when(has_above)
    def _():
        edge_up.wait_send()

    @pl.when(has_next)
    def _():
        fine_down.wait_send()

    @pl.when(has_prev)
    def _():
        fine_up.wait_send()

    @pl.loop(1, nb)
    def _(d):
        k, device = in_b(d)
        swap(0, d, acc.at[k], s1.at[d], device).wait_send()
        swap(2, d, s3.at[beta], s3.at[beta], device).wait_send()

    @pl.loop(1, na)
    def _(d):
        swap(1, d, s2.at[alpha], s2.at[alpha], in_a(d)[1]).wait_send()

    for store in stores + grads:
        store.wait()


def shards(
    nr, nc, fine_in, coarse_in, fine_kernel, coarse_kernel, up_weight, down_weight, fine_cotangent, coarse_cotangent
):
    na, nb = nr // 2, 2 * nc
    vmem, dma = pltpu.VMEM, pltpu.SemaphoreType.DMA
    any_spec = pl.BlockSpec(memory_space=pl.ANY)
    joined_fine, joined_coarse, grad_up, grad_down = pl.pallas_call(
        functools.partial(kernel, nr, nc),
        out_shape=(
            jax.ShapeDtypeStruct((48, 24, 256), BF),
            jax.ShapeDtypeStruct((12, 96, 128), BF),
            jax.ShapeDtypeStruct((48, 96), F32),
            jax.ShapeDtypeStruct((9, 48, 96), F32),
        ),
        in_specs=[any_spec] * 8,
        out_specs=(any_spec,) * 4,
        scratch_shapes=[
            vmem((48, 24, 256), BF),
            vmem((12, 96, 128), BF),
            vmem((9, 48, 48), BF),
            vmem((9, 96, 96), BF),
            vmem((48, 96), BF),
            vmem((9, 48, 96), BF),
            vmem((48, 24, 256), BF),
            vmem((12, 96, 128), BF),
            dma((8,)),
            dma((4,)),
            vmem((3, 144, 240), BF),
            vmem((288, 384), BF),
            vmem((96, 432), BF),
            vmem((98, 16, 128), BF),
            vmem((24, 48, 256), BF),
            vmem((27 * 48, 512), BF),
            vmem((25 * 48, 384), BF),
            vmem((14, 8, 16, 128), BF),
            vmem((6, 96, 256), BF),
            vmem((1152, 256), BF),
            vmem((1152, 256), BF),
            vmem((48, 24, 256), BF),
            vmem((12, 96, 128), BF),
            vmem((48, 96), F32),
            vmem((9, 48, 96), F32),
            vmem((8, 16, 128), BF),
            vmem((8, 16, 128), BF),
            vmem((3, 48, 256), BF),
            vmem((nb, 24, 128), BF),
            vmem((nb, 24, 128), BF),
            vmem((na, 24, 128), BF),
            vmem((nb, 24, 128), BF),
            dma((nc,)),
            dma((nc,)),
            dma((2,)),
            dma((2, nc)),
            dma((2,)),
            dma((2,)),
            dma((3, max(na, nb))),
            dma((3, max(na, nb))),
        ],
        compiler_params=pltpu.CompilerParams(
            collective_id=0, has_side_effects=True, vmem_limit_bytes=40 << 20
        ),
    )(
        fine_in,
        coarse_in,
        fine_kernel,
        coarse_kernel,
        up_weight,
        jnp.swapaxes(down_weight, 1, 2),
        fine_cotangent,
        jnp.swapaxes(coarse_cotangent, 0, 1),
    )
    return joined_fine, jnp.swapaxes(joined_coarse, 0, 1), grad_up, jnp.swapaxes(grad_down, 1, 2)


def solution(mesh):
    strips = P(None, ("rows", "ch"), None)
    return jax.shard_map(
        functools.partial(shards, mesh.shape["rows"], mesh.shape["ch"]),
        mesh=mesh,
        in_specs=(strips, P("ch", "rows", None), P(), P(), P(), P(), strips, strips),
        out_specs=(strips, strips, P(), P()),
        check_vma=False,
    )
```

time: 476 us -> 51.4 us (0.11)
  waiting for transfers between devices: 222 us -> 0 us
  blocking collectives: 81.5 us -> 0 us
  local copies, waits for them, and re-layouts: 76.7 us -> 10.3 us
  matrix products: 54.6 us -> 0 us
  Pallas kernels: 0 us -> 40.1 us
  starting transfers between devices: 20.6 us -> 0 us
  between operations: 14.6 us -> 0.66 us
  other arithmetic: 5.09 us -> 0 us
    psum x1 -> x0, waiting for transfers between devices: 168 us -> none  [shards(): grad_up, grad_down = lax.psum((up_terms, down_terms), ('rows', 'ch'))]
    psum x1 -> x0, blocking collectives: 81.5 us -> none  [shards(): grad_up, grad_down = lax.psum((up_terms, down_terms), ('rows', 'ch'))]
    dot_general x38 -> x0, matrix products: 54.6 us -> none  [the longest x18 48.7 us: conv_rows(): jnp.einsum('oc,chw->ohw', weight[kernel_tap], window, preferred_element_t...]
    slice x12 -> x0, local copies, waits for them, and re-layouts: 54.6 us -> none  [the longest x9 54.5 us: shards(): widened[:, row_shift:row_shift + 2 * coarse_rows - 1:2, col_shift:col_shi...]
    reduce_scatter x1 -> x0, waiting for transfers between devices: 48.5 us -> none  [shards(): lax.psum_scatter(conv_rows(own_kernel, padded_coarse, strip_rows).astype(...]
    pallas_call x0 -> x1, Pallas kernels: none -> 40.1 us  [shards(): pl.pallas_call(functools.partial(kernel, nr, nc), out_shape=(jax.ShapeDty...]
    ppermute x5 -> x0, starting transfers between devices: 16.9 us -> none  [the longest x2 8.06 us: with_halo(): before = lax.ppermute(last, axis, up)]
    convert_element_type x2 -> x0, local copies, waits for them, and re-layouts: 5.76 us -> none  [the longest x1 4.02 us: shards(): conv_rows(own_kernel, padded_coarse, strip_rows).astype(jnp.bfloat16)]
  transfers between devices with their start and end apart: 8 -> 0, of which waited for: 4 -> 0; matrix products, arithmetic and copies ran while one was open for 4% -> 0% of each run, Pallas kernels for 0% -> 0%
where the time goes in v1:
time: 51.4 us; the launch traced here: 51 us
  Pallas kernels  40.1 us (78%)
  local copies, waits for them, and re-layouts  10.3 us (20%)
  between operations  0.66 us (1%)
    pallas_call x1, Pallas kernels, shards(): pl.pallas_call(functools.partial(kernel, nr, nc), out_shape=(jax.ShapeDty...  40.1 us
    unnamed x20, local copies, waits for them, and re-layouts  10.3 us

profile of v1, /device:TPU:1, one launch (start us, length us, event | category | flops | bytes accessed | tf_op | source)
XLA Modules:
  0.0 51.0 jit_solution(18405817956856845730)
XLA Ops:
  0.6 0.0 copy-start
  0.6 1.1 %copy-done = bf16[48,24,256]{2,1,0:T(8,128)(2,1)S(1)} copy-done((bf16[48,24,256]{2,1,0:T(8,128)(2,1)S(1)}, bf16[48,24,256]{2,1,0:T(8,128)(2,1)}, u32[]{:S(2)}) %copy-start) | copy-done | bytes 589848
  1.7 0.0 copy-start.1
  1.7 1.1 %copy-done.1 = bf16[48,24,256]{2,1,0:T(8,128)(2,1)S(1)} copy-done((bf16[48,24,256]{2,1,0:T(8,128)(2,1)S(1)}, bf16[48,24,256]{2,1,0:T(8,128)(2,1)}, u32[]{:S(2)}) %copy-start.1) | copy-done | bytes 589848
  2.8 0.0 copy-start.2
  2.8 1.0 %copy-done.2 = bf16[12,96,128]{2,1,0:T(8,128)(2,1)S(1)} copy-done((bf16[12,96,128]{2,1,0:T(8,128)(2,1)S(1)}, bf16[12,96,128]{2,1,0:T(8,128)(2,1)}, u32[]{:S(2)}) %copy-start.2) | copy-done | bytes 294936
  3.7 0.0 copy-start.3
  3.7 1.0 %copy-done.3 = bf16[96,12,128]{2,0,1:T(8,128)(2,1)S(1)} copy-done((bf16[96,12,128]{2,0,1:T(8,128)(2,1)S(1)}, bf16[96,12,128]{2,0,1:T(8,128)(2,1)}, u32[]{:S(2)}) %copy-start.3) | copy-done | bytes 294936
  4.7 0.0 copy-start.4
  4.7 0.9 %copy-done.4 = bf16[9,96,96]{2,1,0:T(8,128)(2,1)S(1)} copy-done((bf16[9,96,96]{2,1,0:T(8,128)(2,1)S(1)}, bf16[9,96,96]{2,1,0:T(8,128)(2,1)}, u32[]{:S(2)}) %copy-start.4) | copy-done | bytes 165912
  5.6 0.0 copy-start.5
  5.6 0.9 %copy-done.5 = bf16[9,48,48]{2,1,0:T(8,128)(2,1)S(1)} copy-done((bf16[9,48,48]{2,1,0:T(8,128)(2,1)S(1)}, bf16[9,48,48]{2,1,0:T(8,128)(2,1)}, u32[]{:S(2)}) %copy-start.5) | copy-done | bytes 41496
  6.5 0.0 copy-start.6
  6.5 0.9 %copy-done.6 = bf16[9,96,48]{1,2,0:T(8,128)(2,1)S(1)} copy-done((bf16[9,96,48]{1,2,0:T(8,128)(2,1)S(1)}, bf16[9,96,48]{1,2,0:T(8,128)(2,1)}, u32[]{:S(2)}) %copy-start.6) | copy-done | bytes 82968
  7.4 0.0 copy-start.7
  7.4 0.7 %copy-done.7 = bf16[48,96]{1,0:T(8,128)(2,1)S(1)} copy-done((bf16[48,96]{1,0:T(8,128)(2,1)S(1)}, bf16[48,96]{1,0:T(8,128)(2,1)}, u32[]{:S(2)}) %copy-start.7) | copy-done | bytes 9240
  8.1 40.1 %shard_map.111 = (bf16[48,24,256]{2,1,0:T(8,128)(2,1)S(1)}, bf16[12,96,128]{2,1,0:T(8,128)(2,1)S(1)}, f32[48,96]{1,0:T(8,128)S(1)}, f32[9,48,96]{2,1,0:T(8,128)S(1)}) custom-call(bf16[48,24,256]{2,1,0:T(8,128)(2,1)S(1)} %copy-done, bf16[12,96,128]{2,1,0:T(8,128)(2,1)S(1)} %copy-done.2, bf16[9,48,48]{2,1,0:T(8,128)(2,1)S(1)} %copy-done.5, ...), custom_call_target="tpu_custom_call" | custom-call | tf_op jit(solution)/shard_map/pallas_call | solution.py:490
  48.2 0.8 %copy.16 = bf16[48,24,256]{2,1,0:T(8,128)(2,1)} copy(bf16[48,24,256]{2,1,0:T(8,128)(2,1)S(1)} %get-tuple-element.16) | data formatting | bytes 1179648
  49.0 0.7 %copy.17 = bf16[96,12,128]{2,0,1:T(8,128)(2,1)} copy(bf16[96,12,128]{2,0,1:T(8,128)(2,1)S(1)} %bitcast.5) | data formatting | bytes 589824
  49.7 0.6 %copy.18 = f32[48,96]{1,0:T(8,128)} copy(f32[48,96]{1,0:T(8,128)S(1)} %get-tuple-element.18) | data formatting | bytes 36864
  50.3 0.7 %copy.19 = f32[9,96,48]{1,2,0:T(8,128)} copy(f32[9,96,48]{1,2,0:T(8,128)S(1)} %bitcast.6) | data formatting | bytes 331776
Async XLA Ops:
  0.6 1.1 %copy-start = (bf16[48,24,256]{2,1,0:T(8,128)(2,1)S(1)}, bf16[48,24,256]{2,1,0:T(8,128)(2,1)}, u32[]{:S(2)}) copy-start(bf16[48,24,256]{2,1,0:T(8,128)(2,1)} %x_h.1) | copy-start | bytes 1769476
  1.7 1.1 %copy-start.1 = (bf16[48,24,256]{2,1,0:T(8,128)(2,1)S(1)}, bf16[48,24,256]{2,1,0:T(8,128)(2,1)}, u32[]{:S(2)}) copy-start(bf16[48,24,256]{2,1,0:T(8,128)(2,1)} %fcot_h.1) | copy-start | bytes 1769476
  2.8 1.0 %copy-start.2 = (bf16[12,96,128]{2,1,0:T(8,128)(2,1)S(1)}, bf16[12,96,128]{2,1,0:T(8,128)(2,1)}, u32[]{:S(2)}) copy-start(bf16[12,96,128]{2,1,0:T(8,128)(2,1)} %ci_h.1) | copy-start | bytes 884740
  3.7 1.0 %copy-start.3 = (bf16[96,12,128]{2,0,1:T(8,128)(2,1)S(1)}, bf16[96,12,128]{2,0,1:T(8,128)(2,1)}, u32[]{:S(2)}) copy-start(bf16[96,12,128]{2,0,1:T(8,128)(2,1)} %param.15) | copy-start | bytes 884740
  4.7 0.9 %copy-start.4 = (bf16[9,96,96]{2,1,0:T(8,128)(2,1)S(1)}, bf16[9,96,96]{2,1,0:T(8,128)(2,1)}, u32[]{:S(2)}) copy-start(bf16[9,96,96]{2,1,0:T(8,128)(2,1)} %ck_h.1) | copy-start | bytes 497668
  5.6 0.9 %copy-start.5 = (bf16[9,48,48]{2,1,0:T(8,128)(2,1)S(1)}, bf16[9,48,48]{2,1,0:T(8,128)(2,1)}, u32[]{:S(2)}) copy-start(bf16[9,48,48]{2,1,0:T(8,128)(2,1)} %fk_h.1) | copy-start | bytes 124420
  6.5 0.9 %copy-start.6 = (bf16[9,96,48]{1,2,0:T(8,128)(2,1)S(1)}, bf16[9,96,48]{1,2,0:T(8,128)(2,1)}, u32[]{:S(2)}) copy-start(bf16[9,96,48]{1,2,0:T(8,128)(2,1)} %param.13) | copy-start | bytes 248836
  7.4 0.7 %copy-start.7 = (bf16[48,96]{1,0:T(8,128)(2,1)S(1)}, bf16[48,96]{1,0:T(8,128)(2,1)}, u32[]{:S(2)}) copy-start(bf16[48,96]{1,0:T(8,128)(2,1)} %up_h.1) | copy-start | bytes 27652

commit v2 on v1

--- a/solution.py
+++ b/solution.py
@@ -481,22 +481,27 @@
         store.wait()
 
 
+def write_out(*refs):
+    sem = refs[8]
+    copies = [pltpu.make_async_copy(refs[k], refs[4 + k], sem.at[k]) for k in range(4)]
+    for copy in copies:
+        copy.start()
+    for copy in copies:
+        copy.wait()
+
+
 def shards(
     nr, nc, fine_in, coarse_in, fine_kernel, coarse_kernel, up_weight, down_weight, fine_cotangent, coarse_cotangent
 ):
     na, nb = nr // 2, 2 * nc
     vmem, dma = pltpu.VMEM, pltpu.SemaphoreType.DMA
-    any_spec = pl.BlockSpec(memory_space=pl.ANY)
-    joined_fine, joined_coarse, grad_up, grad_down = pl.pallas_call(
+    anywhere = pl.BlockSpec(memory_space=pl.ANY)
+    shapes = [((48, 24, 256), BF), ((12, 96, 128), BF), ((48, 96), F32), ((9, 48, 96), F32)]
+    results = pl.pallas_call(
         functools.partial(kernel, nr, nc),
-        out_shape=(
-            jax.ShapeDtypeStruct((48, 24, 256), BF),
-            jax.ShapeDtypeStruct((12, 96, 128), BF),
-            jax.ShapeDtypeStruct((48, 96), F32),
-            jax.ShapeDtypeStruct((9, 48, 96), F32),
-        ),
-        in_specs=[any_spec] * 8,
-        out_specs=(any_spec,) * 4,
+        out_shape=tuple(vmem(*shape) for shape in shapes),
+        in_specs=[anywhere] * 8,
+        out_specs=(anywhere,) * 4,
         scratch_shapes=[
             vmem((48, 24, 256), BF),
             vmem((12, 96, 128), BF),
@@ -543,15 +548,27 @@
             collective_id=0, has_side_effects=True, vmem_limit_bytes=40 << 20
         ),
     )(
-        fine_in,
-        coarse_in,
-        fine_kernel,
-        coarse_kernel,
-        up_weight,
-        jnp.swapaxes(down_weight, 1, 2),
-        fine_cotangent,
-        jnp.swapaxes(coarse_cotangent, 0, 1),
+        *[
+            pltpu.with_memory_space_constraint(array, pltpu.HBM)
+            for array in (
+                fine_in,
+                coarse_in,
+                fine_kernel,
+                coarse_kernel,
+                up_weight,
+                jnp.swapaxes(down_weight, 1, 2),
+                fine_cotangent,
+                jnp.swapaxes(coarse_cotangent, 0, 1),
+            )
+        ]
     )
+    joined_fine, joined_coarse, grad_up, grad_down = pl.pallas_call(
+        write_out,
+        out_shape=tuple(pltpu.HBM(*shape) for shape in shapes),
+        in_specs=[anywhere] * 4,
+        out_specs=(anywhere,) * 4,
+        scratch_shapes=[dma((4,))],
+    )(*[pltpu.with_memory_space_constraint(array, pltpu.VMEM) for array in results])
     return joined_fine, jnp.swapaxes(joined_coarse, 0, 1), grad_up, jnp.swapaxes(grad_down, 1, 2)
 
 

time: 51.4 us -> 41.1 us (0.80)
  local copies, waits for them, and re-layouts: 10.3 us -> 0 us
    unnamed x20 -> x0, local copies, waits for them, and re-layouts: 10.3 us -> none
    pallas_call x1 -> x2, Pallas kernels: 40.1 us -> 40.3 us  [the longest x1 39.3 us: shards(): pl.pallas_call(functools.partial(kernel, nr, nc), out_shape=tuple((vmem(*...]
where the time goes in v2:
time: 41.1 us; the launch traced here: 41 us
  Pallas kernels  40.3 us (98%)
  between operations  0.64 us (2%)
    pallas_call x1, Pallas kernels, shards(): pl.pallas_call(functools.partial(kernel, nr, nc), out_shape=tuple((vmem(*...  39.3 us
    pallas_call x1, Pallas kernels, shards(): pl.pallas_call(write_out, out_shape=tuple((pltpu.HBM(*shape) for shape in...  1.02 us

profile of v2, /device:TPU:1, one launch (start us, length us, event | category | flops | bytes accessed | tf_op | source)
XLA Modules:
  0.0 41.0 jit_solution(4116126593804075567)
XLA Ops:
  0.6 39.3 %shard_map.111 = (bf16[48,24,256]{2,1,0:T(8,128)(2,1)S(1)}, bf16[12,96,128]{2,1,0:T(8,128)(2,1)S(1)}, f32[48,96]{1,0:T(8,128)S(1)}, f32[9,48,96]{2,1,0:T(8,128)S(1)}) custom-call(bf16[48,24,256]{2,1,0:T(8,128)(2,1)} %x_h.1, bf16[12,96,128]{2,1,0:T(8,128)(2,1)} %ci_h.1, bf16[9,48,48]{2,1,0:T(8,128)(2,1)} %fk_h.1, bf16[9,96,96]{2,1,0:T(8,128)(2,1)} %ck_h.1, ...), custom_call_target="tpu_custom_call" | custom-call | tf_op jit(solution)/shard_map/pallas_call | solution.py:500
  39.9 1.0 %shard_map.112 = (bf16[48,24,256]{2,1,0:T(8,128)(2,1)}, bf16[12,96,128]{2,1,0:T(8,128)(2,1)}, f32[48,96]{1,0:T(8,128)}, f32[9,48,96]{2,1,0:T(8,128)}) custom-call(bf16[48,24,256]{2,1,0:T(8,128)(2,1)S(1)} %get-tuple-element.12.refs_0_, bf16[12,96,128]{2,1,0:T(8,128)(2,1)S(1)} %get-tuple-element.13.refs_1_, f32[48,96]{1,0:T(8,128)S(1)} %get-tuple-element.14.refs_2_, ...), custom_call_target="tpu_custom_call" | custom-call | tf_op jit(solution)/shard_map/pallas_call | solution.py:565

commit v3 on v2

--- a/solution.py
+++ b/solution.py
@@ -2,6 +2,7 @@
 
 import jax
 import jax.numpy as jnp
+import numpy as np
 from jax import lax
 from jax.experimental import pallas as pl
 from jax.experimental.pallas import tpu as pltpu
@@ -64,10 +65,26 @@
 
 
 def prep_coarse(ci, z):
-    v = jnp.concatenate([ci[...], jnp.zeros((4, 96, 128), BF)], axis=0)
-    z[1:97] = jnp.swapaxes(v, 0, 1)
-    z[0] = jnp.zeros((16, 128), BF)
-    z[97] = jnp.zeros((16, 128), BF)
+    order = one_hot(192, 192, lambda r, k: k == (r % 12) * 16 + r // 12)
+    for n in range(3):
+        blocks = [ci[:, 16 * k : 16 * k + 16, :].reshape(192, 128) for k in (2 * n, 2 * n + 1)]
+        out = dot(order, jnp.concatenate(blocks, axis=1)).astype(BF)
+        for k in range(2):
+            at = 16 + 192 * (2 * n + k)
+            z[at : at + 192, :] = out[:, 128 * k : 128 * k + 128]
+    z[0:16, :] = jnp.zeros((16, 128), BF)
+    z[1168:1184, :] = jnp.zeros((16, 128), BF)
+
+
+def place_part(slots, rr, part):
+    (first, count), (row, rows) = PARTS[part], HEIGHTS[part]
+    shift = 4 + 12 * row - first
+    spread = one_hot(16 * rows, count, lambda r, k: (r % 16 < 12) & (k == shift + 12 * (r // 16) + r % 16))
+    for n in range(4):
+        both = [slots[k, first : first + count, :] for k in (2 * n, 2 * n + 1)]
+        out = dot(spread, jnp.concatenate(both, axis=1)).astype(BF)
+        for k in range(2):
+            rr[row : row + rows, 2 * n + k] = out[:, 128 * k : 128 * k + 128].reshape(rows, 16, 128)
 
 
 def spread_fine(rows, u, at):
@@ -99,10 +116,10 @@
     store_features(g, 0, jnp.where(keep, acc, 0.0))
 
 
-def coarse_pair(wc, r, fc, p):
+def coarse_pair(wc, rr, fc, p):
     i = 2 * p
     rows = jnp.concatenate(
-        [r[i : i + 3].reshape(384, 128), r[i + 1 : i + 4].reshape(384, 128)], axis=1
+        [rr[i : i + 3].reshape(384, 128), rr[i + 1 : i + 4].reshape(384, 128)], axis=1
     )
     y = dot(wc[...], rows)
     lane = lax.broadcasted_iota(jnp.int32, (96, 128), 1)
@@ -180,30 +197,42 @@
     grad_up[...] = rows[432:480]
 
 
+def farthest_first(sizes):
+    def hops(digits):
+        total = 0
+        for name, step in zip(sizes, digits):
+            if name == "core":
+                total += 0.1 * step
+            elif name == "x_hi":
+                total += 2 * step
+            elif name == "x_lo":
+                total += step
+            else:
+                total += min(step, sizes[name] - step)
+        return total
+
+    every = [digits for digits in np.ndindex(*sizes.values()) if any(digits)]
+    return sorted(every, key=lambda digits: -hops(digits))
+
+
+SIZES = {"x_hi": 2, "z": 8, "core": 2, "y": 4, "x_lo": 2}
+GROUP_A = {name: SIZES[name] for name in ("z", "core")}
+GROUP_B = {name: SIZES[name] for name in ("x_hi", "y", "x_lo")}
+GROUP_C = {name: SIZES[name] for name in ("y", "x_lo")}
+ORDER_A, ORDER_B, ORDER_C = [farthest_first(group) for group in (GROUP_A, GROUP_B, GROUP_C)]
+NR, NC, NA, NB = 32, 8, 16, 16
+PARTS = ((0, 112), (112, 64))
+HEIGHTS = ((0, 9), (9, 5))
+
+
 def kernel(
-    nr, nc, x_h, ci_h, fk_h, ck_h, up_h, dw_h, fcot_h, ccot_h,
+    x_h, ci_h, fk_h, ck_h, up_h, dw_h, fcot_h, ccot_h,
     jf_o, jc_o, gu_o, gd_o,
     x, ci, fk, ck, up, dw, fcot, ccot, in_sem, out_sem,
-    tb, wc, dm, z, t, u, g, rr, fc, fct, jf, jft, jc, gu_v, gd_v,
+    tb, wc, dm, z, t, u, g, slots, rr, fc, fct, jf, jft, jc, gu_v, gd_v,
     top, bot, hf, acc, s1, s2, s3,
     a2a_s, a2a_r, edge_s, edge_r, fine_s, fine_r, ar_s, ar_r,
 ):
-    r = lax.axis_index("rows")
-    c = lax.axis_index("ch")
-    na = nr // 2
-    nb = 2 * nc
-    alpha = lax.rem(r, na)
-    x_hi = r // na
-    beta = x_hi * nc + c
-
-    def in_a(d):
-        k = lax.rem(alpha + d, na)
-        return k, (x_hi * na + k, c)
-
-    def in_b(d):
-        k = lax.rem(beta + d, nb)
-        return k, ((k // nc) * na + alpha, lax.rem(k, nc))
-
     loads = [
         pltpu.make_async_copy(src, dst, in_sem.at[k])
         for k, (src, dst) in enumerate(
@@ -213,23 +242,42 @@
     for load in loads:
         load.start()
 
+    r = lax.axis_index("rows")
+    c = lax.axis_index("ch")
+    alpha = lax.rem(r, NA)
+    x_hi = r // NA
+    beta = x_hi * NC + c
+    here = {"x_hi": x_hi, "z": alpha // 2, "core": lax.rem(r, 2), "y": c // 2, "x_lo": lax.rem(c, 2)}
+
+    def member(group, digits, sign):
+        at = dict(here)
+        for name, step in zip(group, digits):
+            if step:
+                step = step if sign > 0 else SIZES[name] - step
+                at[name] = lax.rem(at[name] + step, SIZES[name])
+        a = at["z"] * 2 + at["core"]
+        ch = at["y"] * 2 + at["x_lo"]
+        return a, at["x_hi"] * NC + ch, (at["x_hi"] * NA + a, ch)
+
+    ahead_a = [member(GROUP_A, digits, 1) for digits in ORDER_A]
+    ahead_b = [member(GROUP_B, digits, 1) for digits in ORDER_B]
+    ahead_c = [member(GROUP_C, digits, 1) for digits in ORDER_C]
+    back_a = [member(GROUP_A, digits, -1) for digits in ORDER_A]
+    back_b = [member(GROUP_B, digits, -1) for digits in ORDER_B]
+    back_c = [member(GROUP_C, digits, -1) for digits in ORDER_C]
+
     barrier = pltpu.get_barrier_semaphore()
 
     def greet(device):
         pl.semaphore_signal(barrier, inc=1, device_id=device, device_id_type=MESH)
 
-    @pl.loop(1, na)
-    def _(d):
-        greet(in_a(d)[1])
-
-    @pl.loop(1, nb)
-    def _(d):
-        greet(in_b(d)[1])
-
-    first_row, last_row = r == 0, r == nr - 1
+    first_row, last_row = r == 0, r == NR - 1
     has_above, has_below = jnp.logical_not(first_row), jnp.logical_not(last_row)
     is_first = jnp.logical_and(c == 0, has_above)
-    is_last = jnp.logical_and(c == nc - 1, has_below)
+    is_last = jnp.logical_and(c == NC - 1, has_below)
+
+    for _, _, device in ahead_b:
+        greet(device)
 
     @pl.when(has_below)
     def _():
@@ -237,47 +285,47 @@
 
     @pl.when(has_above)
     def _():
-        greet((r - 1, nc - 1))
+        greet((r - 1, NC - 1))
 
     @pl.when(is_first)
     def _():
-        @pl.loop(0, nc)
-        def _(k):
+        for k in range(NC):
             greet((r - 1, k))
 
     @pl.when(is_last)
     def _():
-        @pl.loop(0, nc)
-        def _(k):
+        for k in range(NC):
             greet((r + 1, k))
+
+    for _, _, device in ahead_a:
+        greet(device)
 
     loads[0].wait()
     prep_coarse(ci, z)
-    rr[:, pl.ds(c, 1)] = z[pl.ds(12 * c, 14)].reshape(14, 1, 16, 128)
-    loads[1].wait()
-    t[...] = jnp.swapaxes(x[...], 0, 1)
 
     one = jnp.int32(1)
     zero = jnp.int32(0)
-    peers = na + nb - 2
+    peers = NA + NB - 2
     peers = peers + jnp.where(has_below, one, zero) + jnp.where(has_above, one, zero)
-    peers = peers + jnp.where(is_first, nc * one, zero) + jnp.where(is_last, nc * one, zero)
+    peers = peers + jnp.where(is_first, NC * one, zero) + jnp.where(is_last, NC * one, zero)
     pl.semaphore_wait(barrier, peers)
 
-    def a2a(d):
-        peer = lax.rem(c + d, nc)
+    def a2a(part, n, row, slot, device):
+        first, count = PARTS[part]
         return pltpu.make_async_remote_copy(
-            src_ref=z.at[pl.ds(12 * peer, 14)],
-            dst_ref=rr.at[:, c],
-            send_sem=a2a_s.at[d],
-            recv_sem=a2a_r.at[d],
-            device_id=(r, peer),
+            src_ref=z.at[pl.ds(pl.multiple_of(144 * row + first, 16), count)],
+            dst_ref=slots.at[slot, pl.ds(first, count)],
+            send_sem=a2a_s.at[part, n],
+            recv_sem=a2a_r.at[part, n],
+            device_id=device,
             device_id_type=MESH,
         )
 
-    @pl.loop(1, nc)
-    def _(d):
-        a2a(d).start()
+    sends = [
+        a2a(part, n, device[1], c, device) for part in range(2) for n, (_, _, device) in enumerate(ahead_c)
+    ]
+    for copy in sends[:7]:
+        copy.start()
 
     def edge(k, src, dst, device):
         return pltpu.make_async_remote_copy(
@@ -285,8 +333,8 @@
             device_id=device, device_id_type=MESH,
         )
 
-    edge_down = edge(0, z.at[96], top.at[c], (r + 1, 0))
-    edge_up = edge(1, z.at[1], bot.at[c], (r - 1, nc - 1))
+    edge_down = edge(0, z.at[pl.ds(1152, 16)], top.at[c], (r + 1, 0))
+    edge_up = edge(1, z.at[pl.ds(16, 16)], bot.at[c], (r - 1, NC - 1))
 
     @pl.when(has_below)
     def _():
@@ -296,12 +344,12 @@
     def _():
         edge_up.start()
 
-    wraps_down = c == nc - 1
+    wraps_down = c == NC - 1
     wraps_up = c == 0
     has_next = jnp.logical_not(jnp.logical_and(wraps_down, last_row))
     has_prev = jnp.logical_not(jnp.logical_and(wraps_up, first_row))
-    next_dev = (r + jnp.where(wraps_down, one, zero), lax.rem(c + 1, nc))
-    prev_dev = (r - jnp.where(wraps_up, one, zero), lax.rem(c + nc - 1, nc))
+    next_dev = (r + jnp.where(wraps_down, one, zero), lax.rem(c + 1, NC))
+    prev_dev = (r - jnp.where(wraps_up, one, zero), lax.rem(c + NC - 1, NC))
 
     def halo(k, src, dst, device):
         return pltpu.make_async_remote_copy(
@@ -309,6 +357,8 @@
             device_id=device, device_id_type=MESH,
         )
 
+    loads[1].wait()
+    t[...] = jnp.swapaxes(x[...], 0, 1)
     fine_down = halo(0, t.at[pl.ds(22, 2)], hf.at[pl.ds(0, 2)], next_dev)
     fine_up = halo(1, t.at[pl.ds(0, 1)], hf.at[pl.ds(2, 1)], prev_dev)
 
@@ -319,6 +369,10 @@
     @pl.when(has_prev)
     def _():
         fine_up.start()
+
+    for copy in sends[7:]:
+        copy.start()
+    slots[pl.ds(c, 1)] = z[pl.ds(pl.multiple_of(144 * c, 16), 176), :].reshape(1, 176, 128)
 
     for load in loads[2:5]:
         load.wait()
@@ -332,125 +386,102 @@
         jnp.swapaxes(fcot[...], 0, 1).reshape(1152, 256), split_columns()[:, 128:384]
     ).astype(BF)
 
-    @pl.when(has_prev)
-    def _():
-        fine_down.wait_recv()
-        spread_fine(hf[0:2], u, 0)
-
-    @pl.when(jnp.logical_not(has_prev))
-    def _():
-        u[0:96, :] = jnp.zeros((96, 512), BF)
-
-    @pl.when(has_next)
-    def _():
-        fine_up.wait_recv()
-        spread_fine(hf[2:3], u, 26)
-
-    @pl.when(jnp.logical_not(has_next))
-    def _():
-        u[26 * 48 : 27 * 48, :] = jnp.zeros((48, 512), BF)
-
-    fine_before(tb, u, g, has_prev)
-    fine_group(tb, u, g, 0)
-    fine_group(tb, u, g, 7)
-
-    @pl.loop(1, nc)
-    def _(d):
-        source = lax.rem(c - d + nc, nc)
-        pltpu.make_async_remote_copy(
-            src_ref=z.at[pl.ds(0, 14)],
-            dst_ref=rr.at[:, source],
-            send_sem=a2a_s.at[d],
-            recv_sem=a2a_r.at[d],
-            device_id=(r, source),
-            device_id_type=MESH,
-        ).wait_recv()
-
     def edge_wait(k, buf, row):
-        @pl.loop(0, nc)
-        def _(j):
+        for j in range(NC):
             pltpu.make_async_remote_copy(
-                src_ref=z.at[0], dst_ref=buf.at[j], send_sem=edge_s.at[k], recv_sem=edge_r.at[k, j],
+                src_ref=z.at[pl.ds(0, 16)], dst_ref=buf.at[j], send_sem=edge_s.at[k], recv_sem=edge_r.at[k, j],
                 device_id=(r, c), device_id_type=MESH,
             ).wait_recv()
-
-        rr[row] = buf[...]
-
-    @pl.when(is_first)
-    def _():
-        edge_wait(0, top, 0)
-
-    @pl.when(is_last)
-    def _():
-        edge_wait(1, bot, 13)
-
-    for p in range(6):
-        coarse_pair(wc, rr, fc, p)
+        for j in range(NC):
+            slots[j, row : row + 16, :] = buf[j]
+
     gu = gd = None
-    for p in range(6):
-        a, b = join_pair(up, dm, g, fc, fct, ccot, jf, jc, p)
-        gu = a if gu is None else gu + a
-        gd = b if gd is None else gd + b
+    for part in range(2):
+        for n, (_, _, device) in reversed(list(enumerate(back_c))):
+            a2a(part, n, c, device[1], device).wait_recv()
+
+        if part == 0:
+            pl.when(is_first)(functools.partial(edge_wait, 0, top, 0))
+        else:
+            pl.when(is_last)(functools.partial(edge_wait, 1, bot, 160))
+
+        place_part(slots, rr, part)
+        for p in range(3 * part, 3 * part + 3):
+            coarse_pair(wc, rr, fc, p)
+
+        if part == 0:
+
+            @pl.when(has_prev)
+            def _():
+                fine_down.wait_recv()
+                spread_fine(hf[0:2], u, 0)
+
+            @pl.when(jnp.logical_not(has_prev))
+            def _():
+                u[0:96, :] = jnp.zeros((96, 512), BF)
+
+            @pl.when(has_next)
+            def _():
+                fine_up.wait_recv()
+                spread_fine(hf[2:3], u, 26)
+
+            @pl.when(jnp.logical_not(has_next))
+            def _():
+                u[26 * 48 : 27 * 48, :] = jnp.zeros((48, 512), BF)
+
+            fine_before(tb, u, g, has_prev)
+            fine_group(tb, u, g, 0)
+            fine_group(tb, u, g, 7)
+
+        for p in range(3 * part, 3 * part + 3):
+            a, b = join_pair(up, dm, g, fc, fct, ccot, jf, jc, p)
+            gu = a if gu is None else gu + a
+            gd = b if gd is None else gd + b
 
     acc[...] = pack(gu, gd).astype(acc.dtype)
 
-    def swap(stage, d, src, dst, device):
+    def swap(stage, n, src, dst, device):
         return pltpu.make_async_remote_copy(
-            src_ref=src, dst_ref=dst, send_sem=ar_s.at[stage, d], recv_sem=ar_r.at[stage, d],
+            src_ref=src, dst_ref=dst, send_sem=ar_s.at[stage, n], recv_sem=ar_r.at[stage, n],
             device_id=device, device_id_type=MESH,
         )
 
-    @pl.loop(1, nb)
-    def _(d):
-        k, device = in_b(d)
-        swap(0, d, acc.at[k], s1.at[d], device).start()
+    scatter = [swap(0, n, acc.at[k], s1.at[n], device) for n, (_, k, device) in enumerate(ahead_b)]
+    for copy in scatter:
+        copy.start()
 
     stores = [pltpu.make_async_copy(jft, jf_o, out_sem.at[0]), pltpu.make_async_copy(jc, jc_o, out_sem.at[1])]
     stores[1].start()
     jft[...] = jnp.swapaxes(dot(jf[...], join_columns()).astype(BF).reshape(24, 48, 256), 0, 1)
     stores[0].start()
 
-    @pl.loop(1, nb)
-    def _(d):
-        swap(0, d, acc.at[0], s1.at[d], (r, c)).wait_recv()
-
     part = acc[beta].astype(F32)
-    for d in range(1, nb):
-        part = part + s1[d].astype(F32)
+    for n in reversed(range(NB - 1)):
+        swap(0, n, acc.at[beta], s1.at[n], back_b[n][2]).wait_recv()
+        part = part + s1[n].astype(F32)
     s2[alpha] = part.astype(s2.dtype)
 
-    @pl.loop(1, na)
-    def _(d):
-        swap(1, d, s2.at[alpha], s2.at[alpha], in_a(d)[1]).start()
-
-    @pl.loop(1, na)
-    def _(d):
-        k = lax.rem(alpha - d + na, na)
-        swap(1, d, s2.at[alpha], s2.at[k], (r, c)).wait_recv()
-
+    middle = [swap(1, n, s2.at[alpha], s2.at[alpha], device) for n, (_, _, device) in enumerate(ahead_a)]
+    for copy in middle:
+        copy.start()
+    for n in reversed(range(NA - 1)):
+        swap(1, n, s2.at[alpha], s2.at[back_a[n][0]], back_a[n][2]).wait_recv()
     part = s2[0].astype(F32)
-    for k in range(1, na):
+    for k in range(1, NA):
         part = part + s2[k].astype(F32)
     s3[beta] = part.astype(s3.dtype)
 
-    @pl.loop(1, nb)
-    def _(d):
-        swap(2, d, s3.at[beta], s3.at[beta], in_b(d)[1]).start()
-
-    @pl.loop(1, nb)
-    def _(d):
-        k = lax.rem(beta - d + nb, nb)
-        swap(2, d, s3.at[beta], s3.at[k], (r, c)).wait_recv()
+    gather = [swap(2, n, s3.at[beta], s3.at[beta], device) for n, (_, _, device) in enumerate(ahead_b)]
+    for copy in gather:
+        copy.start()
+    for n in reversed(range(NB - 1)):
+        swap(2, n, s3.at[beta], s3.at[back_b[n][1]], back_b[n][2]).wait_recv()
 
     unpack(s3[...].astype(F32), gu_v, gd_v)
     grads = [pltpu.make_async_copy(gu_v, gu_o, out_sem.at[2]), pltpu.make_async_copy(gd_v, gd_o, out_sem.at[3])]
     for store in grads:
         store.start()
 
-    @pl.loop(1, nc)
-    def _(d):
-        a2a(d).wait_send()
-
     @pl.when(has_below)
     def _():
         edge_down.wait_send()
@@ -467,16 +498,8 @@
     def _():
         fine_up.wait_send()
 
-    @pl.loop(1, nb)
-    def _(d):
-        k, device = in_b(d)
-        swap(0, d, acc.at[k], s1.at[d], device).wait_send()
-        swap(2, d, s3.at[beta], s3.at[beta], device).wait_send()
-
-    @pl.loop(1, na)
-    def _(d):
-        swap(1, d, s2.at[alpha], s2.at[alpha], in_a(d)[1]).wait_send()
-
+    for copy in sends + scatter + middle + gather:
+        copy.wait_send()
     for store in stores + grads:
         store.wait()
 
@@ -491,14 +514,13 @@
 
 
 def shards(
-    nr, nc, fine_in, coarse_in, fine_kernel, coarse_kernel, up_weight, down_weight, fine_cotangent, coarse_cotangent
+    fine_in, coarse_in, fine_kernel, coarse_kernel, up_weight, down_weight, fine_cotangent, coarse_cotangent
 ):
-    na, nb = nr // 2, 2 * nc
     vmem, dma = pltpu.VMEM, pltpu.SemaphoreType.DMA
     anywhere = pl.BlockSpec(memory_space=pl.ANY)
     shapes = [((48, 24, 256), BF), ((12, 96, 128), BF), ((48, 96), F32), ((9, 48, 96), F32)]
     results = pl.pallas_call(
-        functools.partial(kernel, nr, nc),
+        kernel,
         out_shape=tuple(vmem(*shape) for shape in shapes),
         in_specs=[anywhere] * 8,
         out_specs=(anywhere,) * 4,
@@ -516,10 +538,11 @@
             vmem((3, 144, 240), BF),
             vmem((288, 384), BF),
             vmem((96, 432), BF),
-            vmem((98, 16, 128), BF),
+            vmem((1184, 128), BF),
             vmem((24, 48, 256), BF),
             vmem((27 * 48, 512), BF),
             vmem((25 * 48, 384), BF),
+            vmem((8, 176, 128), BF),
             vmem((14, 8, 16, 128), BF),
             vmem((6, 96, 256), BF),
             vmem((1152, 256), BF),
@@ -531,18 +554,18 @@
             vmem((8, 16, 128), BF),
             vmem((8, 16, 128), BF),
             vmem((3, 48, 256), BF),
-            vmem((nb, 24, 128), BF),
-            vmem((nb, 24, 128), BF),
-            vmem((na, 24, 128), BF),
-            vmem((nb, 24, 128), BF),
-            dma((nc,)),
-            dma((nc,)),
+            vmem((NB, 24, 128), BF),
+            vmem((NB, 24, 128), BF),
+            vmem((NA, 24, 128), BF),
+            vmem((NB, 24, 128), BF),
+            dma((2, NC)),
+            dma((2, NC)),
             dma((2,)),
-            dma((2, nc)),
+            dma((2, NC)),
             dma((2,)),
             dma((2,)),
-            dma((3, max(na, nb))),
-            dma((3, max(na, nb))),
+            dma((3, 16)),
+            dma((3, 16)),
         ],
         compiler_params=pltpu.CompilerParams(
             collective_id=0, has_side_effects=True, vmem_limit_bytes=40 << 20
@@ -575,7 +598,7 @@
 def solution(mesh):
     strips = P(None, ("rows", "ch"), None)
     return jax.shard_map(
-        functools.partial(shards, mesh.shape["rows"], mesh.shape["ch"]),
+        shards,
         mesh=mesh,
         in_specs=(strips, P("ch", "rows", None), P(), P(), P(), P(), strips, strips),
         out_specs=(strips, strips, P(), P()),

time: 41.1 us -> 38 us (0.925)
  Pallas kernels: 40.3 us -> 37.3 us
    pallas_call x1, Pallas kernels: 39.3 us -> 36.3 us  [shards(): pl.pallas_call(kernel, out_shape=tuple((vmem(*shape) for shape in shapes)...]
where the time goes in v3:
time: 38 us; the launch traced here: 37.9 us
  Pallas kernels  37.3 us (98%)
  between operations  0.64 us (2%)
    pallas_call x1, Pallas kernels, shards(): pl.pallas_call(kernel, out_shape=tuple((vmem(*shape) for shape in shapes)...  36.3 us
    pallas_call x1, Pallas kernels, shards(): pl.pallas_call(write_out, out_shape=tuple((pltpu.HBM(*shape) for shape in...  1.02 us

profile of v3, /device:TPU:1, one launch (start us, length us, event | category | flops | bytes accessed | tf_op | source)
XLA Modules:
  0.0 37.9 jit_solution(12375732288129798502)
XLA Ops:
  0.6 36.3 %shard_map.111 = (bf16[48,24,256]{2,1,0:T(8,128)(2,1)S(1)}, bf16[12,96,128]{2,1,0:T(8,128)(2,1)S(1)}, f32[48,96]{1,0:T(8,128)S(1)}, f32[9,48,96]{2,1,0:T(8,128)S(1)}) custom-call(bf16[48,24,256]{2,1,0:T(8,128)(2,1)} %x_h.1, bf16[12,96,128]{2,1,0:T(8,128)(2,1)} %ci_h.1, bf16[9,48,48]{2,1,0:T(8,128)(2,1)} %fk_h.1, bf16[9,96,96]{2,1,0:T(8,128)(2,1)} %ck_h.1, ...), custom_call_target="tpu_custom_call" | custom-call | tf_op jit(solution)/shard_map/pallas_call | solution.py:522
  36.9 1.0 %shard_map.112 = (bf16[48,24,256]{2,1,0:T(8,128)(2,1)}, bf16[12,96,128]{2,1,0:T(8,128)(2,1)}, f32[48,96]{1,0:T(8,128)}, f32[9,48,96]{2,1,0:T(8,128)}) custom-call(bf16[48,24,256]{2,1,0:T(8,128)(2,1)S(1)} %get-tuple-element.12.refs_0_, bf16[12,96,128]{2,1,0:T(8,128)(2,1)S(1)} %get-tuple-element.13.refs_1_, f32[48,96]{1,0:T(8,128)S(1)} %get-tuple-element.14.refs_2_, ...), custom_call_target="tpu_custom_call" | custom-call | tf_op jit(solution)/shard_map/pallas_call | solution.py:588

commit v4 on v3

--- a/solution.py
+++ b/solution.py
@@ -229,9 +229,9 @@
     x_h, ci_h, fk_h, ck_h, up_h, dw_h, fcot_h, ccot_h,
     jf_o, jc_o, gu_o, gd_o,
     x, ci, fk, ck, up, dw, fcot, ccot, in_sem, out_sem,
-    tb, wc, dm, z, t, u, g, slots, rr, fc, fct, jf, jft, jc, gu_v, gd_v,
+    tb, wc, dm, z, t, u, g, slots, rr, fc, fct, jf, jft, jc,
     top, bot, hf, acc, s1, s2, s3,
-    a2a_s, a2a_r, edge_s, edge_r, fine_s, fine_r, ar_s, ar_r,
+    relay, a2a_s, a2a_r, edge_s, edge_r, fine_s, fine_r, ar_s, ar_r,
 ):
     loads = [
         pltpu.make_async_copy(src, dst, in_sem.at[k])
@@ -297,18 +297,28 @@
         for k in range(NC):
             greet((r + 1, k))
 
-    for _, _, device in ahead_a:
-        greet(device)
+    def along_z(step, flip):
+        core = lax.rem(here["core"] + flip, 2)
+        return (x_hi * NA + lax.rem(here["z"] + step + 8, 8) * 2 + core, c)
+
+    for step, flip in ((0, 1), (1, 0), (-1, 0), (1, 1), (-1, 1)):
+        greet(along_z(step, flip))
 
     loads[0].wait()
     prep_coarse(ci, z)
 
     one = jnp.int32(1)
     zero = jnp.int32(0)
-    peers = NA + NB - 2
+    peers = NB - 1 + 5
     peers = peers + jnp.where(has_below, one, zero) + jnp.where(has_above, one, zero)
     peers = peers + jnp.where(is_first, NC * one, zero) + jnp.where(is_last, NC * one, zero)
     pl.semaphore_wait(barrier, peers)
+
+    def pass_on(stage, step):
+        pl.semaphore_signal(relay.at[stage], inc=1, device_id=along_z(step, 0), device_id_type=MESH)
+
+    pass_on(0, 1)
+    pass_on(0, -1)
 
     def a2a(part, n, row, slot, device):
         first, count = PARTS[part]
@@ -380,6 +390,9 @@
     spread_fine(t[...], u, 2)
     for k in range(1, 7):
         fine_group(tb, u, g, k)
+    pl.semaphore_wait(relay.at[0], 2)
+    pass_on(1, 2)
+    pass_on(1, -2)
     for load in loads[5:]:
         load.wait()
     fct[...] = dot(
@@ -455,15 +468,39 @@
     jft[...] = jnp.swapaxes(dot(jf[...], join_columns()).astype(BF).reshape(24, 48, 256), 0, 1)
     stores[0].start()
 
+    @pl.when(has_below)
+    def _():
+        edge_down.wait_send()
+
+    @pl.when(has_above)
+    def _():
+        edge_up.wait_send()
+
+    @pl.when(has_next)
+    def _():
+        fine_down.wait_send()
+
+    @pl.when(has_prev)
+    def _():
+        fine_up.wait_send()
+
+    for copy in sends:
+        copy.wait_send()
+
     part = acc[beta].astype(F32)
     for n in reversed(range(NB - 1)):
         swap(0, n, acc.at[beta], s1.at[n], back_b[n][2]).wait_recv()
         part = part + s1[n].astype(F32)
     s2[alpha] = part.astype(s2.dtype)
 
+    pl.semaphore_wait(relay.at[1], 2)
     middle = [swap(1, n, s2.at[alpha], s2.at[alpha], device) for n, (_, _, device) in enumerate(ahead_a)]
     for copy in middle:
         copy.start()
+    for copy in scatter:
+        copy.wait_send()
+    for store in stores:
+        store.wait()
     for n in reversed(range(NA - 1)):
         swap(1, n, s2.at[alpha], s2.at[back_a[n][0]], back_a[n][2]).wait_recv()
     part = s2[0].astype(F32)
@@ -474,34 +511,14 @@
     gather = [swap(2, n, s3.at[beta], s3.at[beta], device) for n, (_, _, device) in enumerate(ahead_b)]
     for copy in gather:
         copy.start()
+    for copy in middle:
+        copy.wait_send()
     for n in reversed(range(NB - 1)):
         swap(2, n, s3.at[beta], s3.at[back_b[n][1]], back_b[n][2]).wait_recv()
 
-    unpack(s3[...].astype(F32), gu_v, gd_v)
-    grads = [pltpu.make_async_copy(gu_v, gu_o, out_sem.at[2]), pltpu.make_async_copy(gd_v, gd_o, out_sem.at[3])]
-    for store in grads:
-        store.start()
-
-    @pl.when(has_below)
-    def _():
-        edge_down.wait_send()
-
-    @pl.when(has_above)
-    def _():
-        edge_up.wait_send()
-
-    @pl.when(has_next)
-    def _():
-        fine_down.wait_send()
-
-    @pl.when(has_prev)
-    def _():
-        fine_up.wait_send()
-
-    for copy in sends + scatter + middle + gather:
+    unpack(s3[...].astype(F32), gu_o, gd_o)
+    for copy in gather:
         copy.wait_send()
-    for store in stores + grads:
-        store.wait()
 
 
 def write_out(*refs):
@@ -523,7 +540,7 @@
         kernel,
         out_shape=tuple(vmem(*shape) for shape in shapes),
         in_specs=[anywhere] * 8,
-        out_specs=(anywhere,) * 4,
+        out_specs=(anywhere,) * 2 + (pl.BlockSpec(memory_space=pltpu.VMEM),) * 2,
         scratch_shapes=[
             vmem((48, 24, 256), BF),
             vmem((12, 96, 128), BF),
@@ -549,8 +566,6 @@
             vmem((1152, 256), BF),
             vmem((48, 24, 256), BF),
             vmem((12, 96, 128), BF),
-            vmem((48, 96), F32),
-            vmem((9, 48, 96), F32),
             vmem((8, 16, 128), BF),
             vmem((8, 16, 128), BF),
             vmem((3, 48, 256), BF),
@@ -558,6 +573,7 @@
             vmem((NB, 24, 128), BF),
             vmem((NA, 24, 128), BF),
             vmem((NB, 24, 128), BF),
+            pltpu.SemaphoreType.REGULAR((2,)),
             dma((2, NC)),
             dma((2, NC)),
             dma((2,)),

time: 38 us -> 37.4 us (0.984)
  Pallas kernels: 37.3 us -> 36.7 us
    pallas_call x1, Pallas kernels: 36.3 us -> 35.7 us  [shards(): pl.pallas_call(kernel, out_shape=tuple((vmem(*shape) for shape in shapes)...]
where the time goes in v4:
time: 37.4 us; the launch traced here: 37.3 us
  Pallas kernels  36.7 us (98%)
  between operations  0.64 us (2%)
    pallas_call x1, Pallas kernels, shards(): pl.pallas_call(kernel, out_shape=tuple((vmem(*shape) for shape in shapes)...  35.7 us
    pallas_call x1, Pallas kernels, shards(): pl.pallas_call(write_out, out_shape=tuple((pltpu.HBM(*shape) for shape in...  1.02 us

profile of v4, /device:TPU:1, one launch (start us, length us, event | category | flops | bytes accessed | tf_op | source)
XLA Modules:
  0.0 37.3 jit_solution(10453251027555074381)
XLA Ops:
  0.6 35.7 %shard_map.111 = (bf16[48,24,256]{2,1,0:T(8,128)(2,1)S(1)}, bf16[12,96,128]{2,1,0:T(8,128)(2,1)S(1)}, f32[48,96]{1,0:T(8,128)S(1)}, f32[9,48,96]{2,1,0:T(8,128)S(1)}) custom-call(bf16[48,24,256]{2,1,0:T(8,128)(2,1)} %x_h.1, bf16[12,96,128]{2,1,0:T(8,128)(2,1)} %ci_h.1, bf16[9,48,48]{2,1,0:T(8,128)(2,1)} %fk_h.1, bf16[9,96,96]{2,1,0:T(8,128)(2,1)} %ck_h.1, ...), custom_call_target="tpu_custom_call" | custom-call | tf_op jit(solution)/shard_map/pallas_call | solution.py:539
  36.3 1.0 %shard_map.112 = (bf16[48,24,256]{2,1,0:T(8,128)(2,1)}, bf16[12,96,128]{2,1,0:T(8,128)(2,1)}, f32[48,96]{1,0:T(8,128)}, f32[9,48,96]{2,1,0:T(8,128)}) custom-call(bf16[48,24,256]{2,1,0:T(8,128)(2,1)S(1)} %get-tuple-element.12.refs_0_, bf16[12,96,128]{2,1,0:T(8,128)(2,1)S(1)} %get-tuple-element.13.refs_1_, f32[48,96]{1,0:T(8,128)S(1)} %get-tuple-element.14.refs_2_, ...), custom_call_target="tpu_custom_call" | custom-call | tf_op jit(solution)/shard_map/pallas_call | solution.py:604

commit v5 on v4

--- a/solution.py
+++ b/solution.py
@@ -38,10 +38,10 @@
 def gate(v):
     k, m = 0.7978845608028654, 0.044715
     q = v * v
-    t = jnp.tanh(v * (k + (k * m) * q))
-    half = 0.5 + 0.5 * t
+    h = 0.5 * jnp.tanh(v * (k + (k * m) * q))
+    half = 0.5 + h
     joined = v * half
-    slope = half + (0.5 * v) * (1.0 - t * t) * (k + (3 * k * m) * q)
+    slope = half + joined * (0.5 - h) * (2 * k + (6 * k * m) * q)
     return joined, slope
 
 
@@ -157,15 +157,13 @@
             total = term if total is None else total + term
         pooled.append(total[:, :128] + total[:, 128:])
     pooled = jnp.concatenate(pooled, axis=1).astype(BF)
-    gu = dot_nt(pooled, f)
     w = windows(g, p)
     pre = f.astype(F32) + dot(dm[...], w)
     joined, slope = gate(pre)
     for s in range(2):
         jc[2 * p + s] = joined[:, 128 * s : 128 * s + 128].astype(BF)
     cc = jnp.concatenate([ccot[2 * p], ccot[2 * p + 1]], axis=1).astype(F32)
-    gd = dot_nt(w, (cc * slope).astype(BF))
-    return gu, gd
+    return pooled, f, (cc * slope).astype(BF), w
 
 
 def pack(gu, gd):
@@ -446,10 +444,13 @@
             fine_group(tb, u, g, 0)
             fine_group(tb, u, g, 7)
 
-        for p in range(3 * part, 3 * part + 3):
-            a, b = join_pair(up, dm, g, fc, fct, ccot, jf, jc, p)
-            gu = a if gu is None else gu + a
-            gd = b if gd is None else gd + b
+        terms = [
+            join_pair(up, dm, g, fc, fct, ccot, jf, jc, p) for p in range(3 * part, 3 * part + 3)
+        ]
+        pooled, f, slope, taps = [jnp.concatenate(term, axis=1) for term in zip(*terms)]
+        a, b = dot_nt(pooled, f), dot_nt(taps, slope)
+        gu = a if gu is None else gu + a
+        gd = b if gd is None else gd + b
 
     acc[...] = pack(gu, gd).astype(acc.dtype)
 

time: 37.4 us -> 37.9 us (1.013)
  Pallas kernels: 36.7 us -> 37.1 us
    pallas_call x1, Pallas kernels: 35.7 us -> 36.1 us  [shards(): pl.pallas_call(kernel, out_shape=tuple((vmem(*shape) for shape in shapes)...]
where the time goes in v5:
time: 37.9 us; the launch traced here: 37.8 us
  Pallas kernels  37.1 us (98%)
  between operations  0.64 us (2%)
    pallas_call x1, Pallas kernels, shards(): pl.pallas_call(kernel, out_shape=tuple((vmem(*shape) for shape in shapes)...  36.1 us
    pallas_call x1, Pallas kernels, shards(): pl.pallas_call(write_out, out_shape=tuple((pltpu.HBM(*shape) for shape in...  1.02 us

profile of v5, /device:TPU:1, one launch (start us, length us, event | category | flops | bytes accessed | tf_op | source)
XLA Modules:
  0.0 37.8 jit_solution(4335504752392776184)
XLA Ops:
  0.6 36.1 %shard_map.111 = (bf16[48,24,256]{2,1,0:T(8,128)(2,1)S(1)}, bf16[12,96,128]{2,1,0:T(8,128)(2,1)S(1)}, f32[48,96]{1,0:T(8,128)S(1)}, f32[9,48,96]{2,1,0:T(8,128)S(1)}) custom-call(bf16[48,24,256]{2,1,0:T(8,128)(2,1)} %x_h.1, bf16[12,96,128]{2,1,0:T(8,128)(2,1)} %ci_h.1, bf16[9,48,48]{2,1,0:T(8,128)(2,1)} %fk_h.1, bf16[9,96,96]{2,1,0:T(8,128)(2,1)} %ck_h.1, ...), custom_call_target="tpu_custom_call" | custom-call | tf_op jit(solution)/shard_map/pallas_call | solution.py:540
  36.7 1.0 %shard_map.112 = (bf16[48,24,256]{2,1,0:T(8,128)(2,1)}, bf16[12,96,128]{2,1,0:T(8,128)(2,1)}, f32[48,96]{1,0:T(8,128)}, f32[9,48,96]{2,1,0:T(8,128)}) custom-call(bf16[48,24,256]{2,1,0:T(8,128)(2,1)S(1)} %get-tuple-element.12.refs_0_, bf16[12,96,128]{2,1,0:T(8,128)(2,1)S(1)} %get-tuple-element.13.refs_1_, f32[48,96]{1,0:T(8,128)S(1)} %get-tuple-element.14.refs_2_, ...), custom_call_target="tpu_custom_call" | custom-call | tf_op jit(solution)/shard_map/pallas_call | solution.py:605
